TPU v7x, 512 devices: a whole 4x4x16 slice. The times are simulated.
512 devices in a mesh: ctx: 32 (over y, x, core), tp: 16 (over z).
Axes of the slice: x: 4, y: 4, z: 16, core: 2. Of those that a mesh axis runs over, the one named last changes fastest.
Arguments:
- features: bfloat16 [8192, 3, 4096], P('ctx', None, 'tp'), may hold values from -6 to 6
- short_taps: float32 [3, 3, 4096], P(None, None, 'tp'), may hold values from -3.5 to 3.5
- residues: float32 [16, 256], P(None, 'tp'), may hold values from -1.5 to 1.5
- rates: float32 [16, 256], P(None, 'tp'), may hold values from 3.6621094e-05 to 0.05, as said below
- skip: float32 [4096], P('tp'), may hold values from -4 to 4
- out_weight: bfloat16 [4096, 4096], P(None, 'tp'), may hold values from -0.09375 to 0.09375
Outputs:
- mixed: bfloat16 [8192, 4096], P('ctx', 'tp')
Inputs may be any that keep to these rules, and one draw needn't show every extreme that they name: `rates`: decay rate of one mode of one filter.
All inputs are finite; a program needn't handle non-finite values.
Results may differ from a plain program's by a relative error of at most 0.0049.
Values may be sent and summed in bfloat16 or wider, within the bound.
No kernel may reach another device: no remote copies, remote signals or barrier semaphores. Data moves between devices by JAX's collectives and lax.ppermute only.
A program may use at most 128 MiB of HBM per device.

v0:
```python
import math

import jax
import jax.numpy as jnp
from jax import lax
from jax.sharding import PartitionSpec as P

SHORT = 3


def passed_along(array, axis, by):
    count = lax.axis_size(axis)
    pairs = [(i, i + by) for i in range(count) if 0 <= i + by < count]
    return lax.ppermute(array, axis, pairs)


def regroup(block):
    return lax.all_to_all(block, "ctx", split_axis=0, concat_axis=0, tiled=True)


def mixdot(form, left, right):
    return jnp.einsum(form, left, right, precision=lax.Precision.HIGHEST)


def rotate(real_part, imag_part, cosine, sine, sign):
    return (
        real_part * cosine - sign * imag_part * sine,
        imag_part * cosine + sign * real_part * sine,
    )


def phase_table(numer, denom):
    angle = 2.0 * math.pi / denom * numer.astype(jnp.float32)
    return (jnp.cos(angle), jnp.sin(angle))


def filter_spectrum(residues, rates, own, rows, ctx_count):
    twice = 2 * ctx_count
    seq_len = rows * ctx_count
    total_len = 2 * seq_len
    sub_index = jnp.arange(2, dtype=jnp.int32)[:, None]
    freq_index = jnp.arange(rows, dtype=jnp.int32)[None, :]
    wave = 2 * own + sub_index + twice * freq_index
    signed = jnp.where(wave < seq_len, wave, wave - total_len)
    theta = 2.0 * math.pi / total_len * signed.astype(jnp.float32)
    theta = theta[None, :, :, None]
    decay = rates[:, None, None, :]
    damping = jnp.exp(-decay)
    den_real = -jnp.expm1(-decay) + damping * 2.0 * jnp.sin(0.5 * theta) ** 2
    den_imag = damping * jnp.sin(theta)
    parity = (1 - 2 * sub_index).astype(jnp.float32)[None, :, :, None]
    numer = 1.0 - jnp.exp(-decay * float(seq_len)) * parity
    scaled = (
        residues[:, None, None, :]
        * jnp.sqrt(2.0 * decay)
        * numer
        / (den_real * den_real + den_imag * den_imag)
    )
    return (jnp.sum(scaled * den_real, axis=0), -jnp.sum(scaled * den_imag, axis=0))


def transform_conv(product, residues, rates, ctx_count, own):
    rows = product.shape[0]
    width = product.shape[1]
    filters = residues.shape[1]
    piece = rows // ctx_count
    twice = 2 * ctx_count
    total_len = 2 * rows * ctx_count
    dev_index = jnp.arange(ctx_count, dtype=jnp.int32)
    freq_group = jnp.arange(twice, dtype=jnp.int32)
    cos_outer, sin_outer = phase_table(freq_group[:, None] * dev_index[None, :] % twice, twice)
    local_pos = own * piece + jnp.arange(piece, dtype=jnp.int32)
    cos_twist, sin_twist = phase_table(
        freq_group[:, None] * local_pos[None, :] % total_len, total_len
    )
    cos_twist = cos_twist[:, :, None]
    sin_twist = sin_twist[:, :, None]
    row_index = jnp.arange(rows, dtype=jnp.int32)
    cos_inner, sin_inner = phase_table(row_index[:, None] * row_index[None, :] % rows, rows)
    cos_inner = cos_inner.reshape(rows, ctx_count, piece)
    sin_inner = sin_inner.reshape(rows, ctx_count, piece)
    moved = regroup(product.reshape(ctx_count, piece, width))
    spec_real = mixdot("ca,ajm->cjm", cos_outer, moved)
    spec_imag = -mixdot("ca,ajm->cjm", sin_outer, moved)
    spec_real, spec_imag = rotate(spec_real, spec_imag, cos_twist, sin_twist, -1.0)
    outgoing = jnp.concatenate([spec_real, spec_imag], -1).reshape(ctx_count, 2 * piece, 2 * width)
    arrived = regroup(outgoing).reshape(ctx_count, 2, piece, 2 * width)
    arr_real = arrived[..., :width]
    arr_imag = arrived[..., width:]
    freq_real = mixdot("usj,scjm->cum", cos_inner, arr_real) + mixdot(
        "usj,scjm->cum", sin_inner, arr_imag
    )
    freq_imag = mixdot("usj,scjm->cum", cos_inner, arr_imag) - mixdot(
        "usj,scjm->cum", sin_inner, arr_real
    )
    filt_real, filt_imag = filter_spectrum(residues, rates, own, rows, ctx_count)
    filt_real = filt_real[..., None]
    filt_imag = filt_imag[..., None]
    freq_real = freq_real.reshape(2, rows, filters, width // filters)
    freq_imag = freq_imag.reshape(2, rows, filters, width // filters)
    prod_real = (freq_real * filt_real - freq_imag * filt_imag).reshape(2, rows, width)
    prod_imag = (freq_real * filt_imag + freq_imag * filt_real).reshape(2, rows, width)
    back_real = mixdot("usj,cum->scjm", cos_inner, prod_real) - mixdot(
        "usj,cum->scjm", sin_inner, prod_imag
    )
    back_imag = mixdot("usj,cum->scjm", sin_inner, prod_real) + mixdot(
        "usj,cum->scjm", cos_inner, prod_imag
    )
    returning = jnp.concatenate([back_real, back_imag], -1).reshape(ctx_count, 2 * piece, 2 * width)
    returned = regroup(returning).reshape(twice, piece, 2 * width)
    ret_real, ret_imag = rotate(
        returned[..., :width], returned[..., width:], cos_twist, sin_twist, 1.0
    )
    scale = 1.0 / total_len
    out_real = mixdot("ca,cjm->ajm", cos_outer, ret_real) - mixdot(
        "ca,cjm->ajm", sin_outer, ret_imag
    )
    time_rows = out_real * scale
    conv = regroup(time_rows).reshape(rows, width)
    return conv


def shards(features, short_taps, residues, rates, skip, out_weight):
    ctx_count = lax.axis_size("ctx")
    own = lax.axis_index("ctx")
    rows = features.shape[0]
    rim = passed_along(features[rows - (SHORT - 1) :], "ctx", 1)
    extended = jnp.concatenate([rim, features], 0)
    shorted = jnp.zeros(features.shape, jnp.float32)
    for shift in range(SHORT):
        window = extended[SHORT - 1 - shift : SHORT - 1 - shift + rows].astype(jnp.float32)
        shorted = shorted + short_taps[shift] * window
    query = shorted[:, 0, :]
    product = shorted[:, 1, :] * shorted[:, 2, :]
    conv = transform_conv(product, residues, rates, ctx_count, own)
    gated = (query * (conv + skip * product)).astype(jnp.bfloat16)
    projected = jnp.dot(
        lax.all_gather(gated, "tp", axis=1, tiled=True),
        out_weight,
        preferred_element_type=jnp.float32,
    )
    return projected.astype(jnp.bfloat16)


def solution(mesh):
    in_specs = (
        P("ctx", None, "tp"),
        P(None, None, "tp"),
        P(None, "tp"),
        P(None, "tp"),
        P("tp"),
        P(None, "tp"),
    )
    out_specs = P("ctx", "tp")
    return jax.shard_map(shards, mesh=mesh, in_specs=in_specs, out_specs=out_specs, check_vma=False)
```

profile of v0, /device:TPU:32, one launch (start us, length us, event | category | flops | bytes accessed | tf_op | source)
XLA Modules:
  0.0 198.4 jit_solution(7042605041022296858)
XLA Ops:
  6.5 0.9 slice.41
  7.4 1.7 collective-permute-start
  9.9 1.8 multiply_add_fusion
  12.5 9.7 %all-to-all-start = ((f32[32,8,256]{2,1,0:T(8,128)}), f32[32,8,256]{2,1,0:T(8,128)S(1)}, u32[]{:S(2)}, u32[]{:S(2)}) async-start(f32[32,8,256]{2,1,0:T(8,128)} %fusion.68), calls=%async_computation | async-start | bytes 524288 | tf_op jit(solution)/shard_map/all_to_all | solution.py:18
  22.3 8.8 %all-to-all-done = f32[32,8,256]{2,1,0:T(8,128)S(1)} async-done(((f32[32,8,256]{2,1,0:T(8,128)}), f32[32,8,256]{2,1,0:T(8,128)S(1)}, u32[]{:S(2)}, u32[]{:S(2)}) %all-to-all-start) | async-done | bytes 262176 | tf_op jit(solution)/shard_map/all_to_all | solution.py:18
  31.8 0.8 multiply_subtract_fusion
  32.8 1.6 copy.36
  34.4 4.7 %all-to-all-start.1 = ((f32[32,16,512]{2,1,0:T(8,128)}), f32[32,16,512]{2,1,0:T(8,128)}, u32[]{:S(2)}, u32[]{:S(2)}) async-start(f32[32,16,512]{2,1,0:T(8,128)} %bitcast.118), calls=%async_computation.1 | async-start | bytes 2097152 | tf_op jit(solution)/shard_map/all_to_all | solution.py:18
  39.9 16.5 %all-to-all-done.1 = f32[32,16,512]{2,1,0:T(8,128)} async-done(((f32[32,16,512]{2,1,0:T(8,128)}), f32[32,16,512]{2,1,0:T(8,128)}, u32[]{:S(2)}, u32[]{:S(2)}) %all-to-all-start.1) | async-done | bytes 1048608 | tf_op jit(solution)/shard_map/all_to_all | solution.py:18
  56.4 1.8 copy.37
  58.2 1.9 convolution_bitcast_fusion.2
  60.1 1.9 convolution_bitcast_fusion
  62.0 1.9 fusion.3
  63.9 1.9 fusion.11
  65.9 1.6 fusion.14
  67.5 1.8 fusion.16
  69.3 1.6 fusion
  70.9 1.6 fusion.1
  73.2 20.6 %all_to_all.20 = f32[32,16,512]{2,1,0:T(8,128)S(1)} all-to-all(f32[32,16,512]{2,1,0:T(8,128)S(1)} %copy.42), channel_id=1, replica_groups=mesh['ctx'=32,'tp'=16] {'ctx'}, dimensions={0} | all-to-all | bytes 2097152 | tf_op jit(solution)/shard_map/all_to_all | solution.py:18
  94.0 0.8 fusion.21
  94.7 0.8 fusion.6
  95.7 12.3 %all_to_all.21 = f32[32,8,256]{2,1,0:T(8,128)S(1)} all-to-all(f32[32,8,256]{2,1,0:T(8,128)S(1)} %copy.45), channel_id=1, replica_groups=mesh['ctx'=32,'tp'=16] {'ctx'}, dimensions={0} | all-to-all | bytes 524288 | tf_op jit(solution)/shard_map/all_to_all | solution.py:18
  108.7 79.9 %all-gather.2.cloned.1.call-done = bf16[256,4096]{1,0:T(8,128)(2,1)} async-done(((bf16[256,256]{1,0:T(8,128)(2,1)}), bf16[256,4096]{1,0:T(8,128)(2,1)}) %all-gather.2.cloned.1.call-update) | async-done | bytes 2097168 | tf_op jit(solution)/shard_map/all_gather | solution.py:138
  188.6 3.0 %convolution_convert_fusion = bf16[256,256]{1,0:T(8,128)(2,1)} fusion(bf16[256,4096]{1,0:T(8,128)(2,1)} %all-gather.2.cloned.1.call-done, bf16[4096,256]{1,0:T(8,128)(2,1)S(1)} %copy-done), kind=kOutput, calls=%fused_computation.15 | convolution fusion | flops 536936448 | bytes 4325376 | tf_op jit(solution)/shard_map/dot_general | solution.py:137
  (31 shorter events, 5.0 us)
Async XLA Ops:
  6.5 182.0 %copy-start = (bf16[4096,256]{1,0:T(8,128)(2,1)S(1)}, bf16[4096,256]{1,0:T(8,128)(2,1)}, u32[]{:S(2)}) copy-start(bf16[4096,256]{1,0:T(8,128)(2,1)} %param.11) | copy-start | bytes 6291460
  7.4 2.5 %collective-permute-start = (bf16[2,3,256]{2,0,1:T(2,128)(2,1)S(1)}, bf16[2,3,256]{2,0,1:T(2,128)(2,1)S(1)}, u32[]{:S(2)}, u32[]{:S(2)}) collective-permute-start(bf16[2,3,256]{2,0,1:T(2,128)(2,1)S(1)} %slice.41), channel_id=1, source_target_pairs={{0,16},{16,32},{32,48},{48,64},{64,80},{80,96},{96,112},{112,128},... | collective-permute-start | bytes 9224 | tf_op jit(solution)/shard_map/ppermute | solution.py:14
  12.5 18.6 %all-to-all-start = ((f32[32,8,256]{2,1,0:T(8,128)}), f32[32,8,256]{2,1,0:T(8,128)S(1)}, u32[]{:S(2)}, u32[]{:S(2)}) async-start(f32[32,8,256]{2,1,0:T(8,128)} %fusion.68), calls=%async_computation | async-start | bytes 524288 | tf_op jit(solution)/shard_map/all_to_all | solution.py:18
  32.8 6.7 %copy-start.1 = (f32[16,16]{1,0:T(8,128)S(1)}, f32[16,16]{1,0:T(8,128)}, u32[]{:S(2)}) copy-start(f32[16,16]{1,0:T(8,128)} %param.8) | copy-start | bytes 3076
  32.8 6.7 %copy-start.2 = (f32[16,16]{1,0:T(8,128)S(1)}, f32[16,16]{1,0:T(8,128)}, u32[]{:S(2)}) copy-start(f32[16,16]{1,0:T(8,128)} %param.9) | copy-start | bytes 3076
  34.4 22.0 %all-to-all-start.1 = ((f32[32,16,512]{2,1,0:T(8,128)}), f32[32,16,512]{2,1,0:T(8,128)}, u32[]{:S(2)}, u32[]{:S(2)}) async-start(f32[32,16,512]{2,1,0:T(8,128)} %bitcast.118), calls=%async_computation.1 | async-start | bytes 2097152 | tf_op jit(solution)/shard_map/all_to_all | solution.py:18
  39.1 149.5 %all-gather.2.cloned.1.call-start = ((), (), s32[]{:S(2)}) async-start(), calls=%async_computation.4 | async-start | bytes 2228224 | tf_op jit(solution)/shard_map/all_gather | solution.py:138
  94.0 14.0 %copy-start.3 = (f32[256]{0:T(256)S(1)}, f32[256]{0:T(256)}, u32[]{:S(2)}) copy-start(f32[256]{0:T(256)} %param.10) | copy-start | bytes 3076
Sparse Core Ops, SparseCore 0:
  108.8 79.7 all-gather.1
where the time goes:
time: 199 us; the launch traced here: 198 us
  waiting for transfers between devices  105 us (53%)
  blocking collectives  32.9 us (17%)
  matrix products  20.2 us (10%)
  starting transfers between devices  16.3 us (8%)
  between operations  13.7 us (7%)
  local copies, waits for them, and re-layouts  5.9 us (3%)
  other arithmetic  4.2 us (2%)
    all_gather x1, waiting for transfers between devices, shards(): lax.all_gather(gated, 'tp', axis=1, tiled=True)  79.9 us
    all_to_all x2, blocking collectives, regroup(): return lax.all_to_all(block, 'ctx', split_axis=0, concat_axis=0, tiled=True)  32.9 us
    all_to_all x2, waiting for transfers between devices, regroup(): return lax.all_to_all(block, 'ctx', split_axis=0, concat_axis=0, tiled=True)  25.2 us
    dot_general x12, matrix products, mixdot(): return jnp.einsum(form, left, right, precision=lax.Precision.HIGHEST)  17.2 us
    all_to_all x2, starting transfers between devices, regroup(): return lax.all_to_all(block, 'ctx', split_axis=0, concat_axis=0, tiled=True)  14.4 us
  transfers between devices with their start and end apart: 4, of which 4 were waited for; matrix products, arithmetic and copies ran while one was open for 1% of the time, Pallas kernels for 0%

commit v1 on v0

v1 whole, which is shorter than its diff:
```python
import functools

import jax
import jax.numpy as jnp
from jax import lax
from jax.experimental import pallas as pl
from jax.experimental.pallas import tpu as pltpu
from jax.sharding import PartitionSpec as P

SHORT = 3
CHUNKS = 8
RIM = 16
LANES = 128
HIGHEST = lax.Precision.HIGHEST


def per_channel(table, width):
    filters = table.shape[1]
    group = width // filters
    row = lax.broadcasted_iota(jnp.int32, (filters, width), 0)
    col = lax.broadcasted_iota(jnp.int32, (filters, width), 1)
    pick = jnp.where(col // group == row, 1.0, 0.0).astype(jnp.float32)
    return lax.dot_general(
        table, pick, (((1,), (0,)), ((), ())), precision=HIGHEST,
        preferred_element_type=jnp.float32,
    )


def short_filter(block, taps, before_last, last):
    row = lax.broadcasted_iota(jnp.int32, block.shape, 0)
    one = jnp.where(row == 0, last, pltpu.roll(block, 1, 0))
    two = jnp.where(row == 0, before_last, jnp.where(row == 1, last, pltpu.roll(block, 2, 0)))
    return taps[0] * block + taps[1] * one + taps[2] * two


def save(ref, array):
    rows, width = array.shape
    for t in range(width // LANES):
        ref[pl.ds(t * rows, rows), :] = array[:, t * LANES : (t + 1) * LANES]


def strided(ref, rows, width, start, count, stride):
    return jnp.concatenate(
        [ref[pl.ds(t * rows + start, count, stride=stride), :] for t in range(width // LANES)], 1
    )


def spread(table, r, t):
    return jnp.broadcast_to(table[r : r + 1, t * LANES : (t + 1) * LANES], (CHUNKS, LANES))


def recur(product_ref, base, decay, states, steps, visit=None):
    def step(i, carry):
        now = product_ref[pl.ds(base + i, CHUNKS, stride=steps), :]
        carry = tuple(d * h + now for d, h in zip(decay, carry))
        if visit is not None:
            visit(i, carry)
        return carry

    return lax.fori_loop(0, steps, step, states, unroll=4)


def chunk_ends(product_ref, ends_ref, lam, rows):
    modes, width = lam.shape
    decay = jnp.exp(-lam)
    for t in range(width // LANES):
        blank = tuple(jnp.zeros((CHUNKS, LANES), jnp.float32) for _ in range(modes))
        part = [spread(decay, r, t) for r in range(modes)]
        ends = recur(product_ref, t * rows, part, blank, rows // CHUNKS)
        for r, end in enumerate(ends):
            ends_ref[pl.ds((t * modes + r) * CHUNKS, CHUNKS), :] = end


def state_kernel(feat_ref, taps_ref, rates_ref, send_ref, product_ref, ends_ref):
    rows, width = feat_ref.shape[1:]
    modes = rates_ref.shape[0]
    lam = per_channel(rates_ref[...], width)
    zero = jnp.zeros((1, width), jnp.float32)
    keys, values = (
        short_filter(
            feat_ref[j].astype(jnp.float32), [taps_ref[s, j : j + 1, :] for s in range(SHORT)],
            zero, zero,
        )
        for j in (1, 2)
    )
    row = lax.broadcasted_iota(jnp.int32, (rows, width), 0)
    save(product_ref, jnp.where(row < SHORT - 1, 0.0, keys * values))
    chunk_ends(product_ref, ends_ref, lam, rows)
    over_chunk = jnp.exp(-lam * float(rows // CHUNKS))
    total = jnp.zeros((modes, width), jnp.float32)
    for j in range(CHUNKS):
        end = strided(ends_ref, modes * CHUNKS, width, j, modes, CHUNKS)
        total = total * over_chunk + end
    head = [feat_ref[j, 0:2, :].astype(jnp.float32) for j in (1, 2)]
    tail = [feat_ref[j, rows - 2 : rows, :].astype(jnp.float32) for j in (1, 2, 0)]
    rim = jnp.concatenate(head + tail + [jnp.zeros((RIM - 10, width), jnp.float32)], 0)
    block = jnp.concatenate([total, rim], 0).astype(jnp.bfloat16)
    for e in range(send_ref.shape[0]):
        send_ref[e] = block


def gate_kernel(
    recv_ref, feat_ref, taps_ref, rates_ref, residues_ref, skip_ref, out_ref,
    rims_ref, product_ref, states_ref, conv_ref,
):
    blocks = recv_ref.shape[0]
    rows, width = feat_ref.shape[1:]
    modes = rates_ref.shape[0]
    steps = rows // CHUNKS
    own = lax.axis_index("ctx")
    lam = per_channel(rates_ref[...], width)
    coef = per_channel(residues_ref[...] * jnp.sqrt(2.0 * rates_ref[...]), width)
    taps = [[taps_ref[s, j : j + 1, :] for s in range(SHORT)] for j in range(3)]

    for e in range(blocks):
        edges = recv_ref[e, pl.ds(modes, RIM), :].astype(jnp.float32)
        for t in range(width // LANES):
            rims_ref[pl.ds((t * blocks + e) * RIM, RIM), :] = edges[:, t * LANES : (t + 1) * LANES]

    def edge(k):
        return strided(rims_ref, blocks * RIM, width, k, blocks, RIM)

    block_row = lax.broadcasted_iota(jnp.int32, (blocks, width), 0)

    def earlier(k):
        return jnp.where(block_row == 0, 0.0, pltpu.roll(edge(k), 1, 0))

    def firsts(j, head, tail):
        zeroth, first = edge(head), edge(head + 1)
        before_last, last = earlier(tail), earlier(tail + 1)
        a, b, c = taps[j]
        return a * zeroth + b * last + c * before_last, a * first + b * zeroth + c * last

    key0, key1 = firsts(1, 0, 4)
    value0, value1 = firsts(2, 2, 6)
    product0, product1 = key0 * value0, key1 * value1

    over_block = jnp.exp(-lam * float(rows))
    weight0 = jnp.exp(-lam * float(rows - 1))
    weight1 = jnp.exp(-lam * float(rows - 2))
    state = jnp.zeros((modes, width), jnp.float32)
    for e in range(blocks - 1):
        added = (
            recv_ref[e, pl.ds(0, modes), :].astype(jnp.float32)
            + weight0 * product0[e : e + 1]
            + weight1 * product1[e : e + 1]
        )
        state = jnp.where(e < own, state * over_block + added, state)

    previous = jnp.maximum(own - 1, 0)
    tails = recv_ref[previous, pl.ds(modes, RIM), :].astype(jnp.float32)
    tails = jnp.where(own > 0, tails, 0.0)
    query, keys, values = (
        short_filter(
            feat_ref[j].astype(jnp.float32), taps[j], tails[k : k + 1], tails[k + 1 : k + 2]
        )
        for j, k in ((0, 8), (1, 4), (2, 6))
    )
    product = keys * values
    save(product_ref, product)

    chunk_ends(product_ref, states_ref, lam, rows)
    over_chunk = jnp.exp(-lam * float(steps))
    for j in range(CHUNKS):
        end = strided(states_ref, modes * CHUNKS, width, j, modes, CHUNKS)
        for t in range(width // LANES):
            where = pl.ds(t * modes * CHUNKS + j, modes, stride=CHUNKS)
            states_ref[where, :] = state[:, t * LANES : (t + 1) * LANES]
        state = state * over_chunk + end

    decay = jnp.exp(-lam)
    for t in range(width // LANES):
        part = [spread(decay, r, t) for r in range(modes)]
        scale = [spread(coef, r, t) for r in range(modes)]
        begin = tuple(
            states_ref[pl.ds((t * modes + r) * CHUNKS, CHUNKS), :] for r in range(modes)
        )

        def visit(i, carry, t=t, scale=scale):
            total = functools.reduce(jnp.add, [s * h for s, h in zip(scale, carry)])
            conv_ref[pl.ds(t * rows + i, CHUNKS, stride=steps), :] = total

        recur(product_ref, t * rows, part, begin, steps, visit)

    conv = jnp.concatenate(
        [conv_ref[pl.ds(t * rows, rows), :] for t in range(width // LANES)], 1
    )
    gated = query * (conv + skip_ref[...] * product)
    gated = gated.astype(jnp.bfloat16).astype(jnp.float32)
    root = jnp.sqrt(jnp.sqrt(jnp.abs(gated) * 2.0**32))
    out_ref[...] = jnp.where(gated < 0.0, -root, root)


def shards(features, short_taps, residues, rates, skip, out_weight):
    blocks = lax.axis_size("ctx")
    rows, _, width = features.shape
    modes = rates.shape[0]
    feats = features.transpose(1, 0, 2)
    f32 = jnp.float32
    tiles = width // LANES
    sent = pl.pallas_call(
        state_kernel,
        out_shape=jax.ShapeDtypeStruct((blocks, modes + RIM, width), jnp.bfloat16),
        scratch_shapes=[
            pltpu.VMEM((tiles * rows, LANES), f32),
            pltpu.VMEM((tiles * modes * CHUNKS, LANES), f32),
        ],
        name="block_state",
    )(feats, short_taps, rates)
    received = lax.all_to_all(sent, "ctx", split_axis=0, concat_axis=0, tiled=True)
    coded = pl.pallas_call(
        gate_kernel,
        out_shape=jax.ShapeDtypeStruct((rows, width), f32),
        scratch_shapes=[
            pltpu.VMEM((tiles * blocks * RIM, LANES), f32),
            pltpu.VMEM((tiles * rows, LANES), f32),
            pltpu.VMEM((tiles * modes * CHUNKS, LANES), f32),
            pltpu.VMEM((tiles * rows, LANES), f32),
        ],
        name="conv_gate",
    )(received, feats, short_taps, rates, residues, skip.reshape(1, width))
    gathered = lax.all_gather(coded.astype(jnp.float16), "tp", axis=1, tiled=True).astype(f32)
    square = gathered * gathered
    gated = (square * (gathered * jnp.abs(gathered)) * 2.0**-32).astype(jnp.bfloat16)
    return jnp.dot(gated, out_weight, preferred_element_type=f32).astype(jnp.bfloat16)


def solution(mesh):
    in_specs = (
        P("ctx", None, "tp"),
        P(None, None, "tp"),
        P(None, "tp"),
        P(None, "tp"),
        P("tp"),
        P(None, "tp"),
    )
    return jax.shard_map(
        shards, mesh=mesh, in_specs=in_specs, out_specs=P("ctx", "tp"), check_vma=False
    )
```

time: 199 us -> 78.6 us (0.39)
  the two profiles are of different devices: /device:TPU:32 before, /device:TPU:2 now
where the time goes in v1:
time: 78.6 us; the launch traced here: 78.3 us
  blocking collectives  68.3 us (87%)
  Pallas kernels  7.32 us (9%)
  matrix products  1.7 us (2%)
  other arithmetic  0.97 us (1%)
    all_gather x1, blocking collectives, shards(): lax.all_gather(coded.astype(jnp.float16), 'tp', axis=1, tiled=True)  47.6 us
    all_to_all x1, blocking collectives, shards(): lax.all_to_all(sent, 'ctx', split_axis=0, concat_axis=0, tiled=True)  20.8 us
    pallas_call x1, Pallas kernels, shards(): pl.pallas_call(gate_kernel, out_shape=jax.ShapeDtypeStruct((rows, width),...  4.38 us
    pallas_call x1, Pallas kernels, shards(): pl.pallas_call(state_kernel, out_shape=jax.ShapeDtypeStruct((blocks, mode...  2.94 us
    dot_general x1, matrix products, shards(): jnp.dot(gated, out_weight, preferred_element_type=f32).astype(jnp.bfloat16)  1.7 us

profile of v1, /device:TPU:2, one launch (start us, length us, event | category | flops | bytes accessed | tf_op | source)
XLA Modules:
  0.0 78.3 jit_solution(17547128778096024717)
XLA Ops:
  0.0 0.0 copy-start
  0.0 2.9 %block_state.1 = bf16[32,32,256]{2,1,0:T(8,128)(2,1)} custom-call(bf16[3,256,256]{2,1,0:T(8,128)(2,1)} %bitcast.3, f32[3,3,256]{2,1,0:T(4,128)} %taps_ref.3, f32[16,16]{1,0:T(8,128)} %rates_ref.3), custom_call_target="tpu_custom_call" | custom-call | tf_op jit(solution)/shard_map/block_state/pallas_call | solution.py:201
  2.9 20.8 %all_to_all.5.recv_ref = bf16[32,32,256]{2,1,0:T(8,128)(2,1)} all-to-all(bf16[32,32,256]{2,1,0:T(8,128)(2,1)} %block_state.1), channel_id=1, replica_groups=mesh['ctx'=32,'tp'=16] {'ctx'}, dimensions={0} | all-to-all | bytes 1048576 | tf_op jit(solution)/shard_map/all_to_all | solution.py:210
  23.7 4.4 %conv_gate.1 = f32[256,256]{1,0:T(8,128)} custom-call(bf16[32,32,256]{2,1,0:T(8,128)(2,1)} %all_to_all.5.recv_ref, bf16[3,256,256]{2,1,0:T(8,128)(2,1)} %bitcast.4, f32[3,3,256]{2,1,0:T(4,128)} %taps_ref.3, f32[16,16]{1,0:T(8,128)} %rates_ref.3, f32[16,16]{1,0:T(8,128)} %residues_ref.1, f32[1,256]{1,0:T(1,128)} %bitcast.5), custom_call_target="tpu_custom_call" | custom-call | tf_op jit(solution)/shard_map/conv_gate/pallas_call | solution.py:211
  28.1 1.0 %convert_element_type.12 = f16[256,256]{1,0:T(8,128)(2,1)S(1)} convert(f32[256,256]{1,0:T(8,128)} %conv_gate.1) | non-fusion elementwise | flops 65536 | bytes 393216 | tf_op jit(solution)/shard_map/convert_element_type | solution.py:222
  29.0 47.6 %all-gather.1 = f16[256,4096]{1,0:T(8,128)(2,1)S(1)} all-gather(f16[256,256]{1,0:T(8,128)(2,1)S(1)} %convert_element_type.12), channel_id=1, replica_groups=mesh['ctx'=32,'tp'=16] {'tp'}, dimensions={1}, use_global_device_ids=true | all-gather | bytes 2228224 | tf_op jit(solution)/shard_map/all_gather | solution.py:222
  76.6 0.0 copy-done
  76.6 1.7 %fusion.5 = bf16[256,256]{1,0:T(8,128)(2,1)} fusion(bf16[4096,256]{1,0:T(8,128)(2,1)S(1)} %copy-done, f16[256,4096]{1,0:T(8,128)(2,1)S(1)} %all-gather.1), kind=kOutput, calls=%fused_computation.6 | convolution fusion | flops 544276480 | bytes 4325376 | tf_op jit(solution)/shard_map/dot_general | solution.py:225
Async XLA Ops:
  0.0 76.6 %copy-start = (bf16[4096,256]{1,0:T(8,128)(2,1)S(1)}, bf16[4096,256]{1,0:T(8,128)(2,1)}, u32[]{:S(2)}) copy-start(bf16[4096,256]{1,0:T(8,128)(2,1)} %param.11) | copy-start | bytes 6291460

commit v2 on v1

--- a/solution.py
+++ b/solution.py
@@ -45,6 +45,10 @@
     )
 
 
+def whole(ref, rows, width):
+    return jnp.concatenate([ref[pl.ds(t * rows, rows), :] for t in range(width // LANES)], 1)
+
+
 def spread(table, r, t):
     return jnp.broadcast_to(table[r : r + 1, t * LANES : (t + 1) * LANES], (CHUNKS, LANES))
 
@@ -71,20 +75,26 @@
             ends_ref[pl.ds((t * modes + r) * CHUNKS, CHUNKS), :] = end
 
 
+def channel_taps(taps_ref, j):
+    return [taps_ref[s, j : j + 1, :] for s in range(SHORT)]
+
+
+def inner_product(feat_ref, taps_ref):
+    rows, width = feat_ref.shape[1:]
+    zero = jnp.zeros((1, width), jnp.float32)
+    keys, values = (
+        short_filter(feat_ref[j].astype(jnp.float32), channel_taps(taps_ref, j), zero, zero)
+        for j in (1, 2)
+    )
+    row = lax.broadcasted_iota(jnp.int32, (rows, width), 0)
+    return jnp.where(row < SHORT - 1, 0.0, keys * values)
+
+
 def state_kernel(feat_ref, taps_ref, rates_ref, send_ref, product_ref, ends_ref):
     rows, width = feat_ref.shape[1:]
     modes = rates_ref.shape[0]
     lam = per_channel(rates_ref[...], width)
-    zero = jnp.zeros((1, width), jnp.float32)
-    keys, values = (
-        short_filter(
-            feat_ref[j].astype(jnp.float32), [taps_ref[s, j : j + 1, :] for s in range(SHORT)],
-            zero, zero,
-        )
-        for j in (1, 2)
-    )
-    row = lax.broadcasted_iota(jnp.int32, (rows, width), 0)
-    save(product_ref, jnp.where(row < SHORT - 1, 0.0, keys * values))
+    save(product_ref, inner_product(feat_ref, taps_ref))
     chunk_ends(product_ref, ends_ref, lam, rows)
     over_chunk = jnp.exp(-lam * float(rows // CHUNKS))
     total = jnp.zeros((modes, width), jnp.float32)
@@ -93,24 +103,65 @@
         total = total * over_chunk + end
     head = [feat_ref[j, 0:2, :].astype(jnp.float32) for j in (1, 2)]
     tail = [feat_ref[j, rows - 2 : rows, :].astype(jnp.float32) for j in (1, 2, 0)]
-    rim = jnp.concatenate(head + tail + [jnp.zeros((RIM - 10, width), jnp.float32)], 0)
+    own_query = [feat_ref[0, 0:2, :].astype(jnp.float32)]
+    blank = [jnp.zeros((RIM - 12, width), jnp.float32)]
+    rim = jnp.concatenate(head + tail + own_query + blank, 0)
     block = jnp.concatenate([total, rim], 0).astype(jnp.bfloat16)
     for e in range(send_ref.shape[0]):
         send_ref[e] = block
 
 
-def gate_kernel(
-    recv_ref, feat_ref, taps_ref, rates_ref, residues_ref, skip_ref, out_ref,
-    rims_ref, product_ref, states_ref, conv_ref,
+def local_kernel(
+    feat_ref, taps_ref, rates_ref, residues_ref, skip_ref, query_ref, base_ref,
+    product_ref, states_ref, conv_ref,
+):
+    rows, width = feat_ref.shape[1:]
+    modes = rates_ref.shape[0]
+    steps = rows // CHUNKS
+    lam = per_channel(rates_ref[...], width)
+    coef = per_channel(residues_ref[...] * jnp.sqrt(2.0 * rates_ref[...]), width)
+    zero = jnp.zeros((1, width), jnp.float32)
+    query = short_filter(feat_ref[0].astype(jnp.float32), channel_taps(taps_ref, 0), zero, zero)
+    product = inner_product(feat_ref, taps_ref)
+    save(product_ref, product)
+    chunk_ends(product_ref, states_ref, lam, rows)
+    over_chunk = jnp.exp(-lam * float(steps))
+    state = jnp.zeros((modes, width), jnp.float32)
+    for j in range(CHUNKS):
+        end = strided(states_ref, modes * CHUNKS, width, j, modes, CHUNKS)
+        for t in range(width // LANES):
+            where = pl.ds(t * modes * CHUNKS + j, modes, stride=CHUNKS)
+            states_ref[where, :] = state[:, t * LANES : (t + 1) * LANES]
+        state = state * over_chunk + end
+    decay = jnp.exp(-lam)
+    for t in range(width // LANES):
+        part = [spread(decay, r, t) for r in range(modes)]
+        scale = [spread(coef, r, t) for r in range(modes)]
+        begin = tuple(
+            states_ref[pl.ds((t * modes + r) * CHUNKS, CHUNKS), :] for r in range(modes)
+        )
+
+        def visit(i, carry, t=t, scale=scale):
+            total = functools.reduce(jnp.add, [s * h for s, h in zip(scale, carry)])
+            conv_ref[pl.ds(t * rows + i, CHUNKS, stride=steps), :] = total
+
+        recur(product_ref, t * rows, part, begin, steps, visit)
+    query_ref[...] = query
+    base_ref[...] = query * (whole(conv_ref, rows, width) + skip_ref[...] * product)
+
+
+def carry_kernel(
+    recv_ref, query_ref, base_ref, taps_ref, rates_ref, residues_ref, skip_ref, out_ref,
+    rims_ref, firsts_ref, states_ref, conv_ref,
 ):
     blocks = recv_ref.shape[0]
-    rows, width = feat_ref.shape[1:]
+    rows, width = query_ref.shape
     modes = rates_ref.shape[0]
     steps = rows // CHUNKS
     own = lax.axis_index("ctx")
     lam = per_channel(rates_ref[...], width)
     coef = per_channel(residues_ref[...] * jnp.sqrt(2.0 * rates_ref[...]), width)
-    taps = [[taps_ref[s, j : j + 1, :] for s in range(SHORT)] for j in range(3)]
+    skip = skip_ref[...]
 
     for e in range(blocks):
         edges = recv_ref[e, pl.ds(modes, RIM), :].astype(jnp.float32)
@@ -128,12 +179,18 @@
     def firsts(j, head, tail):
         zeroth, first = edge(head), edge(head + 1)
         before_last, last = earlier(tail), earlier(tail + 1)
-        a, b, c = taps[j]
+        a, b, c = channel_taps(taps_ref, j)
         return a * zeroth + b * last + c * before_last, a * first + b * zeroth + c * last
 
+    query0, query1 = firsts(0, 10, 8)
     key0, key1 = firsts(1, 0, 4)
     value0, value1 = firsts(2, 2, 6)
     product0, product1 = key0 * value0, key1 * value1
+    for k, array in enumerate((query0, query1, product0, product1)):
+        firsts_ref[pl.ds(k * blocks, blocks), :] = array
+    own_query0, own_query1, own_product0, own_product1 = (
+        firsts_ref[pl.ds(k * blocks + own, 1), :] for k in range(4)
+    )
 
     over_block = jnp.exp(-lam * float(rows))
     weight0 = jnp.exp(-lam * float(rows - 1))
@@ -147,45 +204,39 @@
         )
         state = jnp.where(e < own, state * over_block + added, state)
 
-    previous = jnp.maximum(own - 1, 0)
-    tails = recv_ref[previous, pl.ds(modes, RIM), :].astype(jnp.float32)
-    tails = jnp.where(own > 0, tails, 0.0)
-    query, keys, values = (
-        short_filter(
-            feat_ref[j].astype(jnp.float32), taps[j], tails[k : k + 1], tails[k + 1 : k + 2]
-        )
-        for j, k in ((0, 8), (1, 4), (2, 6))
-    )
-    product = keys * values
-    save(product_ref, product)
-
-    chunk_ends(product_ref, states_ref, lam, rows)
-    over_chunk = jnp.exp(-lam * float(steps))
+    decay = jnp.exp(-lam)
+    state0 = decay * state + own_product0
+    state1 = decay * state0 + own_product1
+    gated0, gated1 = (
+        q * (jnp.sum(coef * h, 0, keepdims=True) + skip * p)
+        for q, h, p in (
+            (own_query0, state0, own_product0), (own_query1, state1, own_product1)
+        )
+    )
+
+    grow = jnp.exp(lam)
+    start = coef * (state + grow * (own_product0 + grow * own_product1))
     for j in range(CHUNKS):
-        end = strided(states_ref, modes * CHUNKS, width, j, modes, CHUNKS)
+        scaled = start * jnp.exp(-lam * float(steps * j))
         for t in range(width // LANES):
             where = pl.ds(t * modes * CHUNKS + j, modes, stride=CHUNKS)
-            states_ref[where, :] = state[:, t * LANES : (t + 1) * LANES]
-        state = state * over_chunk + end
-
-    decay = jnp.exp(-lam)
+            states_ref[where, :] = scaled[:, t * LANES : (t + 1) * LANES]
     for t in range(width // LANES):
         part = [spread(decay, r, t) for r in range(modes)]
-        scale = [spread(coef, r, t) for r in range(modes)]
         begin = tuple(
             states_ref[pl.ds((t * modes + r) * CHUNKS, CHUNKS), :] for r in range(modes)
         )
 
-        def visit(i, carry, t=t, scale=scale):
-            total = functools.reduce(jnp.add, [s * h for s, h in zip(scale, carry)])
-            conv_ref[pl.ds(t * rows + i, CHUNKS, stride=steps), :] = total
-
-        recur(product_ref, t * rows, part, begin, steps, visit)
-
-    conv = jnp.concatenate(
-        [conv_ref[pl.ds(t * rows, rows), :] for t in range(width // LANES)], 1
-    )
-    gated = query * (conv + skip_ref[...] * product)
+        def step(i, carry, t=t, part=part):
+            carry = tuple(d * h for d, h in zip(part, carry))
+            where = pl.ds(t * rows + i, CHUNKS, stride=steps)
+            conv_ref[where, :] = functools.reduce(jnp.add, carry)
+            return carry
+
+        lax.fori_loop(0, steps, step, begin, unroll=4)
+    gated = base_ref[...] + query_ref[...] * whole(conv_ref, rows, width)
+    row = lax.broadcasted_iota(jnp.int32, (rows, width), 0)
+    gated = jnp.where(row == 0, gated0, jnp.where(row == 1, gated1, gated))
     gated = gated.astype(jnp.bfloat16).astype(jnp.float32)
     root = jnp.sqrt(jnp.sqrt(jnp.abs(gated) * 2.0**32))
     out_ref[...] = jnp.where(gated < 0.0, -root, root)
@@ -196,29 +247,36 @@
     rows, _, width = features.shape
     modes = rates.shape[0]
     feats = features.transpose(1, 0, 2)
+    skip = skip.reshape(1, width)
     f32 = jnp.float32
     tiles = width // LANES
+    plane = jax.ShapeDtypeStruct((rows, width), f32)
+    by_row = pltpu.VMEM((tiles * rows, LANES), f32)
+    by_mode = pltpu.VMEM((tiles * modes * CHUNKS, LANES), f32)
     sent = pl.pallas_call(
         state_kernel,
         out_shape=jax.ShapeDtypeStruct((blocks, modes + RIM, width), jnp.bfloat16),
-        scratch_shapes=[
-            pltpu.VMEM((tiles * rows, LANES), f32),
-            pltpu.VMEM((tiles * modes * CHUNKS, LANES), f32),
-        ],
+        scratch_shapes=[by_row, by_mode],
         name="block_state",
     )(feats, short_taps, rates)
     received = lax.all_to_all(sent, "ctx", split_axis=0, concat_axis=0, tiled=True)
+    query, base = pl.pallas_call(
+        local_kernel,
+        out_shape=(plane, plane),
+        scratch_shapes=[by_row, by_mode, by_row],
+        name="local_conv",
+    )(feats, short_taps, rates, residues, skip)
     coded = pl.pallas_call(
-        gate_kernel,
-        out_shape=jax.ShapeDtypeStruct((rows, width), f32),
+        carry_kernel,
+        out_shape=plane,
         scratch_shapes=[
             pltpu.VMEM((tiles * blocks * RIM, LANES), f32),
-            pltpu.VMEM((tiles * rows, LANES), f32),
-            pltpu.VMEM((tiles * modes * CHUNKS, LANES), f32),
-            pltpu.VMEM((tiles * rows, LANES), f32),
+            pltpu.VMEM((4 * blocks, width), f32),
+            by_mode,
+            by_row,
         ],
-        name="conv_gate",
-    )(received, feats, short_taps, rates, residues, skip.reshape(1, width))
+        name="carry_gate",
+    )(received, query, base, short_taps, rates, residues, skip)
     gathered = lax.all_gather(coded.astype(jnp.float16), "tp", axis=1, tiled=True).astype(f32)
     square = gathered * gathered
     gated = (square * (gathered * jnp.abs(gathered)) * 2.0**-32).astype(jnp.bfloat16)

time: 78.6 us -> 78 us (level)
  blocking collectives: 68.3 us -> 48.2 us
  starting transfers between devices: 0 us -> 9.45 us
  waiting for transfers between devices: 0 us -> 6.74 us
  Pallas kernels: 7.32 us -> 9.87 us
  local copies, waits for them, and re-layouts: 0.01 us -> 0.8 us
    all_to_all x1 -> x0, blocking collectives: 20.8 us -> none  [shards(): lax.all_to_all(sent, 'ctx', split_axis=0, concat_axis=0, tiled=True)]
    all_to_all x0 -> x1, starting transfers between devices: none -> 9.45 us  [shards(): lax.all_to_all(sent, 'ctx', split_axis=0, concat_axis=0, tiled=True)]
    all_to_all x0 -> x1, waiting for transfers between devices: none -> 6.74 us  [shards(): lax.all_to_all(sent, 'ctx', split_axis=0, concat_axis=0, tiled=True)]
    pallas_call x1 -> x2, Pallas kernels: 4.38 us -> 6.96 us  [the longest x1 3.86 us: shards(): pl.pallas_call(local_kernel, out_shape=(plane, plane), scratch_shapes=[by...]
    unnamed x2 -> x4, local copies, waits for them, and re-layouts: 0.01 us -> 0.8 us
  transfers between devices with their start and end apart: 0 -> 1, of which waited for: 0 -> 1; matrix products, arithmetic and copies ran while one was open for 0% -> 0% of each run, Pallas kernels for 0% -> 5%
where the time goes in v2:
time: 78 us; the launch traced here: 77.7 us
  blocking collectives  48.2 us (62%)
  Pallas kernels  9.87 us (13%)
  starting transfers between devices  9.45 us (12%)
  waiting for transfers between devices  6.74 us (9%)
  matrix products  1.7 us (2%)
  other arithmetic  0.97 us (1%)
  local copies, waits for them, and re-layouts  0.8 us (1%)
    all_gather x1, blocking collectives, shards(): lax.all_gather(coded.astype(jnp.float16), 'tp', axis=1, tiled=True)  48.2 us
    all_to_all x1, starting transfers between devices, shards(): lax.all_to_all(sent, 'ctx', split_axis=0, concat_axis=0, tiled=True)  9.45 us
    all_to_all x1, waiting for transfers between devices, shards(): lax.all_to_all(sent, 'ctx', split_axis=0, concat_axis=0, tiled=True)  6.74 us
    pallas_call x1, Pallas kernels, shards(): pl.pallas_call(local_kernel, out_shape=(plane, plane), scratch_shapes=[by...  3.86 us
    pallas_call x1, Pallas kernels, shards(): pl.pallas_call(carry_kernel, out_shape=plane, scratch_shapes=[pltpu.VMEM(...  3.1 us
    pallas_call x1, Pallas kernels, shards(): pl.pallas_call(state_kernel, out_shape=jax.ShapeDtypeStruct((blocks, mode...  2.92 us
    dot_general x1, matrix products, shards(): jnp.dot(gated, out_weight, preferred_element_type=f32).astype(jnp.bfloat16)  1.7 us
  transfers between devices with their start and end apart: 1, of which 1 were waited for; matrix products, arithmetic and copies ran while one was open for 0% of the time, Pallas kernels for 5%

profile of v2, /device:TPU:2, one launch (start us, length us, event | category | flops | bytes accessed | tf_op | source)
XLA Modules:
  0.0 77.7 jit_solution(8661217969887126366)
XLA Ops:
  0.0 0.0 copy-start
  0.0 2.9 %block_state.1 = bf16[32,32,256]{2,1,0:T(8,128)(2,1)} custom-call(bf16[3,256,256]{2,1,0:T(8,128)(2,1)} %bitcast.3, f32[3,3,256]{2,1,0:T(4,128)} %taps_ref.5, f32[16,16]{1,0:T(8,128)} %rates_ref.5), custom_call_target="tpu_custom_call" | custom-call | tf_op jit(solution)/shard_map/block_state/pallas_call | solution.py:256
  2.9 9.5 %all-to-all-start = ((bf16[32,32,256]{2,1,0:T(8,128)(2,1)}), bf16[32,32,256]{2,1,0:T(8,128)(2,1)S(1)}, u32[]{:S(2)}, u32[]{:S(2)}) async-start(bf16[32,32,256]{2,1,0:T(8,128)(2,1)} %block_state.1), calls=%async_computation | async-start | bytes 1048576 | tf_op jit(solution)/shard_map/all_to_all | solution.py:262
  12.4 3.9 %local_conv.1 = (f32[256,256]{1,0:T(8,128)}, f32[256,256]{1,0:T(8,128)}) custom-call(bf16[3,256,256]{2,1,0:T(8,128)(2,1)} %bitcast.4, f32[3,3,256]{2,1,0:T(4,128)} %taps_ref.5, f32[16,16]{1,0:T(8,128)} %rates_ref.5, f32[16,16]{1,0:T(8,128)} %residues_ref.3, f32[1,256]{1,0:T(1,128)} %bitcast.5), custom_call_target="tpu_custom_call" | custom-call | tf_op jit(solution)/shard_map/local_conv/pallas_call | solution.py:263
  16.2 6.7 %all-to-all-done.recv_ref = bf16[32,32,256]{2,1,0:T(8,128)(2,1)S(1)} async-done(((bf16[32,32,256]{2,1,0:T(8,128)(2,1)}), bf16[32,32,256]{2,1,0:T(8,128)(2,1)S(1)}, u32[]{:S(2)}, u32[]{:S(2)}) %all-to-all-start) | async-done | bytes 524320 | tf_op jit(solution)/shard_map/all_to_all | solution.py:262
  23.0 0.0 copy-start.1
  23.0 0.8 %copy-done.1 = bf16[32,32,256]{2,1,0:T(8,128)(2,1)} copy-done((bf16[32,32,256]{2,1,0:T(8,128)(2,1)}, bf16[32,32,256]{2,1,0:T(8,128)(2,1)S(1)}, u32[]{:S(2)}) %copy-start.1) | copy-done | bytes 524312
  23.8 3.1 %carry_gate.1 = f32[256,256]{1,0:T(8,128)} custom-call(bf16[32,32,256]{2,1,0:T(8,128)(2,1)} %copy-done.1, f32[256,256]{1,0:T(8,128)} %get-tuple-element.7.query_ref, f32[256,256]{1,0:T(8,128)} %get-tuple-element.8.base_ref, f32[3,3,256]{2,1,0:T(4,128)} %taps_ref.5, f32[16,16]{1,0:T(8,128)} %rates_ref.5, f32[16,16]{1,0:T(8,128)} %residues_ref.3, f32[1,256]{1,0:T(1,128)} %bitcast.6), custom_call_target="tpu_custom_call" | custom-call | tf_op jit(solution)/shard_map/carry_gate/pallas_call | solution.py:269
  26.9 1.0 %convert_element_type.12 = f16[256,256]{1,0:T(8,128)(2,1)S(1)} convert(f32[256,256]{1,0:T(8,128)} %carry_gate.1) | non-fusion elementwise | flops 65536 | bytes 393216 | tf_op jit(solution)/shard_map/convert_element_type | solution.py:280
  27.9 48.2 %all-gather.1 = f16[256,4096]{1,0:T(8,128)(2,1)S(1)} all-gather(f16[256,256]{1,0:T(8,128)(2,1)S(1)} %convert_element_type.12), channel_id=1, replica_groups=mesh['ctx'=32,'tp'=16] {'tp'}, dimensions={1}, use_global_device_ids=true | all-gather | bytes 2228224 | tf_op jit(solution)/shard_map/all_gather | solution.py:280
  76.0 0.0 copy-done
  76.0 1.7 %fusion.5 = bf16[256,256]{1,0:T(8,128)(2,1)} fusion(bf16[4096,256]{1,0:T(8,128)(2,1)S(1)} %copy-done, f16[256,4096]{1,0:T(8,128)(2,1)S(1)} %all-gather.1), kind=kOutput, calls=%fused_computation.6 | convolution fusion | flops 544276480 | bytes 4325376 | tf_op jit(solution)/shard_map/dot_general | solution.py:283
Async XLA Ops:
  0.0 76.0 %copy-start = (bf16[4096,256]{1,0:T(8,128)(2,1)S(1)}, bf16[4096,256]{1,0:T(8,128)(2,1)}, u32[]{:S(2)}) copy-start(bf16[4096,256]{1,0:T(8,128)(2,1)} %param.11) | copy-start | bytes 6291460
  2.9 20.1 %all-to-all-start = ((bf16[32,32,256]{2,1,0:T(8,128)(2,1)}), bf16[32,32,256]{2,1,0:T(8,128)(2,1)S(1)}, u32[]{:S(2)}, u32[]{:S(2)}) async-start(bf16[32,32,256]{2,1,0:T(8,128)(2,1)} %block_state.1), calls=%async_computation | async-start | bytes 1048576 | tf_op jit(solution)/shard_map/all_to_all | solution.py:262
  23.0 0.8 %copy-start.1 = (bf16[32,32,256]{2,1,0:T(8,128)(2,1)}, bf16[32,32,256]{2,1,0:T(8,128)(2,1)S(1)}, u32[]{:S(2)}) copy-start(bf16[32,32,256]{2,1,0:T(8,128)(2,1)S(1)} %all-to-all-done.recv_ref) | copy-start | bytes 1572868

commit v3 on v2

--- a/solution.py
+++ b/solution.py
@@ -11,6 +11,8 @@
 CHUNKS = 8
 RIM = 16
 LANES = 128
+TABLES = 7
+KERNEL_VMEM = 12 * 2**20
 HIGHEST = lax.Precision.HIGHEST
 
 
@@ -90,7 +92,20 @@
     return jnp.where(row < SHORT - 1, 0.0, keys * values)
 
 
-def state_kernel(feat_ref, taps_ref, rates_ref, send_ref, product_ref, ends_ref):
+def state_kernel(
+    feat_hbm, taps_hbm, rates_hbm, send_ref,
+    feat_ref, taps_ref, rates_ref, product_ref, ends_ref, sems,
+):
+    copies = [
+        pltpu.make_async_copy(source, target, sems.at[k])
+        for k, (source, target) in enumerate(
+            ((feat_hbm, feat_ref), (taps_hbm, taps_ref), (rates_hbm, rates_ref))
+        )
+    ]
+    for copy in copies:
+        copy.start()
+    for copy in copies:
+        copy.wait()
     rows, width = feat_ref.shape[1:]
     modes = rates_ref.shape[0]
     lam = per_channel(rates_ref[...], width)
@@ -112,7 +127,7 @@
 
 
 def local_kernel(
-    feat_ref, taps_ref, rates_ref, residues_ref, skip_ref, query_ref, base_ref,
+    feat_ref, taps_ref, rates_ref, residues_ref, skip_ref, local_ref,
     product_ref, states_ref, conv_ref,
 ):
     rows, width = feat_ref.shape[1:]
@@ -146,22 +161,44 @@
             conv_ref[pl.ds(t * rows + i, CHUNKS, stride=steps), :] = total
 
         recur(product_ref, t * rows, part, begin, steps, visit)
-    query_ref[...] = query
-    base_ref[...] = query * (whole(conv_ref, rows, width) + skip_ref[...] * product)
+    for k, table in enumerate(
+        (
+            decay,
+            jnp.exp(lam),
+            jnp.exp(-lam * float(rows - 2)),
+            jnp.exp(-lam * float(rows - 1)),
+            jnp.exp(-lam * float(rows)),
+            over_chunk,
+            coef,
+        )
+    ):
+        local_ref[pl.ds(2 * rows + k * modes, modes), :] = table
+    singles = 2 * rows + TABLES * modes
+    for j in range(3):
+        for shift, tap in enumerate(channel_taps(taps_ref, j)):
+            local_ref[pl.ds(singles + SHORT * j + shift, 1), :] = tap
+    local_ref[pl.ds(singles + 3 * SHORT, 1), :] = skip_ref[...]
+    local_ref[pl.ds(0, rows), :] = query
+    local_ref[pl.ds(rows, rows), :] = query * (whole(conv_ref, rows, width) + skip_ref[...] * product)
 
 
 def carry_kernel(
-    recv_ref, query_ref, base_ref, taps_ref, rates_ref, residues_ref, skip_ref, out_ref,
+    recv_ref, local_ref, out_ref,
     rims_ref, firsts_ref, states_ref, conv_ref,
 ):
     blocks = recv_ref.shape[0]
-    rows, width = query_ref.shape
-    modes = rates_ref.shape[0]
+    rows, width = out_ref.shape
+    modes = recv_ref.shape[1] - RIM
     steps = rows // CHUNKS
     own = lax.axis_index("ctx")
-    lam = per_channel(rates_ref[...], width)
-    coef = per_channel(residues_ref[...] * jnp.sqrt(2.0 * rates_ref[...]), width)
-    skip = skip_ref[...]
+    decay, grow, weight1, weight0, over_block, over_chunk, coef = (
+        local_ref[pl.ds(2 * rows + k * modes, modes), :] for k in range(TABLES)
+    )
+
+    def single(k):
+        return local_ref[pl.ds(2 * rows + TABLES * modes + k, 1), :]
+
+    skip = single(3 * SHORT)
 
     for e in range(blocks):
         edges = recv_ref[e, pl.ds(modes, RIM), :].astype(jnp.float32)
@@ -179,7 +216,7 @@
     def firsts(j, head, tail):
         zeroth, first = edge(head), edge(head + 1)
         before_last, last = earlier(tail), earlier(tail + 1)
-        a, b, c = channel_taps(taps_ref, j)
+        a, b, c = (single(SHORT * j + shift) for shift in range(SHORT))
         return a * zeroth + b * last + c * before_last, a * first + b * zeroth + c * last
 
     query0, query1 = firsts(0, 10, 8)
@@ -192,9 +229,6 @@
         firsts_ref[pl.ds(k * blocks + own, 1), :] for k in range(4)
     )
 
-    over_block = jnp.exp(-lam * float(rows))
-    weight0 = jnp.exp(-lam * float(rows - 1))
-    weight1 = jnp.exp(-lam * float(rows - 2))
     state = jnp.zeros((modes, width), jnp.float32)
     for e in range(blocks - 1):
         added = (
@@ -204,7 +238,6 @@
         )
         state = jnp.where(e < own, state * over_block + added, state)
 
-    decay = jnp.exp(-lam)
     state0 = decay * state + own_product0
     state1 = decay * state0 + own_product1
     gated0, gated1 = (
@@ -214,13 +247,12 @@
         )
     )
 
-    grow = jnp.exp(lam)
     start = coef * (state + grow * (own_product0 + grow * own_product1))
     for j in range(CHUNKS):
-        scaled = start * jnp.exp(-lam * float(steps * j))
         for t in range(width // LANES):
             where = pl.ds(t * modes * CHUNKS + j, modes, stride=CHUNKS)
-            states_ref[where, :] = scaled[:, t * LANES : (t + 1) * LANES]
+            states_ref[where, :] = start[:, t * LANES : (t + 1) * LANES]
+        start = start * over_chunk
     for t in range(width // LANES):
         part = [spread(decay, r, t) for r in range(modes)]
         begin = tuple(
@@ -234,7 +266,8 @@
             return carry
 
         lax.fori_loop(0, steps, step, begin, unroll=4)
-    gated = base_ref[...] + query_ref[...] * whole(conv_ref, rows, width)
+    query, base = local_ref[pl.ds(0, rows), :], local_ref[pl.ds(rows, rows), :]
+    gated = base + query * whole(conv_ref, rows, width)
     row = lax.broadcasted_iota(jnp.int32, (rows, width), 0)
     gated = jnp.where(row == 0, gated0, jnp.where(row == 1, gated1, gated))
     gated = gated.astype(jnp.bfloat16).astype(jnp.float32)
@@ -253,21 +286,36 @@
     plane = jax.ShapeDtypeStruct((rows, width), f32)
     by_row = pltpu.VMEM((tiles * rows, LANES), f32)
     by_mode = pltpu.VMEM((tiles * modes * CHUNKS, LANES), f32)
+    whole_in = pl.BlockSpec(memory_space=pltpu.VMEM)
     sent = pl.pallas_call(
         state_kernel,
+        in_specs=[pl.BlockSpec(memory_space=pltpu.HBM)] * 3,
+        out_specs=whole_in,
         out_shape=jax.ShapeDtypeStruct((blocks, modes + RIM, width), jnp.bfloat16),
-        scratch_shapes=[by_row, by_mode],
+        scratch_shapes=[
+            pltpu.VMEM(feats.shape, feats.dtype),
+            pltpu.VMEM(short_taps.shape, f32),
+            pltpu.VMEM(rates.shape, f32),
+            by_row,
+            by_mode,
+            pltpu.SemaphoreType.DMA((3,)),
+        ],
         name="block_state",
     )(feats, short_taps, rates)
     received = lax.all_to_all(sent, "ctx", split_axis=0, concat_axis=0, tiled=True)
-    query, base = pl.pallas_call(
+    local = pl.pallas_call(
         local_kernel,
-        out_shape=(plane, plane),
+        in_specs=[whole_in] * 5,
+        out_specs=whole_in,
+        out_shape=jax.ShapeDtypeStruct((2 * rows + (TABLES + 1) * modes, width), f32),
         scratch_shapes=[by_row, by_mode, by_row],
+        compiler_params=pltpu.CompilerParams(vmem_limit_bytes=KERNEL_VMEM),
         name="local_conv",
     )(feats, short_taps, rates, residues, skip)
     coded = pl.pallas_call(
         carry_kernel,
+        in_specs=[whole_in] * 2,
+        out_specs=whole_in,
         out_shape=plane,
         scratch_shapes=[
             pltpu.VMEM((tiles * blocks * RIM, LANES), f32),
@@ -275,8 +323,9 @@
             by_mode,
             by_row,
         ],
+        compiler_params=pltpu.CompilerParams(vmem_limit_bytes=KERNEL_VMEM),
         name="carry_gate",
-    )(received, query, base, short_taps, rates, residues, skip)
+    )(received, local)
     gathered = lax.all_gather(coded.astype(jnp.float16), "tp", axis=1, tiled=True).astype(f32)
     square = gathered * gathered
     gated = (square * (gathered * jnp.abs(gathered)) * 2.0**-32).astype(jnp.bfloat16)

time: 78 us -> 74.4 us (0.954)
  Pallas kernels: 9.87 us -> 6.01 us
  local copies, waits for them, and re-layouts: 0.8 us -> 3.77 us
  waiting for transfers between devices: 6.74 us -> 4.75 us
  other arithmetic: 0.97 us -> 0.02 us
    pallas_call x3, Pallas kernels: 9.87 us -> 6.01 us  [the longest x1 2.93 us: shards(): pl.pallas_call(state_kernel, in_specs=[pl.BlockSpec(memory_space=pltpu.HB...]
    unnamed x4 -> x12, local copies, waits for them, and re-layouts: 0.8 us -> 3.77 us
    all_to_all x1, waiting for transfers between devices: 6.74 us -> 4.75 us  [shards(): lax.all_to_all(sent, 'ctx', split_axis=0, concat_axis=0, tiled=True)]
    convert_element_type x1, other arithmetic: 0.97 us -> 0.02 us  [shards(): coded.astype(jnp.float16)]
  transfers between devices with their start and end apart: 1 -> 1, of which waited for: 1 -> 1; matrix products, arithmetic and copies ran while one was open for 0% -> 0% of each run, Pallas kernels for 5% -> 3%
where the time goes in v3:
time: 74.4 us; the launch traced here: 73.9 us
  blocking collectives  48.2 us (65%)
  starting transfers between devices  9.47 us (13%)
  Pallas kernels  6.01 us (8%)
  waiting for transfers between devices  4.75 us (6%)
  local copies, waits for them, and re-layouts  3.77 us (5%)
  matrix products  1.7 us (2%)
    all_gather x1, blocking collectives, shards(): lax.all_gather(coded.astype(jnp.float16), 'tp', axis=1, tiled=True)  48.2 us
    all_to_all x1, starting transfers between devices, shards(): lax.all_to_all(sent, 'ctx', split_axis=0, concat_axis=0, tiled=True)  9.47 us
    all_to_all x1, waiting for transfers between devices, shards(): lax.all_to_all(sent, 'ctx', split_axis=0, concat_axis=0, tiled=True)  4.75 us
    unnamed x12, local copies, waits for them, and re-layouts  3.77 us
    pallas_call x1, Pallas kernels, shards(): pl.pallas_call(state_kernel, in_specs=[pl.BlockSpec(memory_space=pltpu.HB...  2.93 us
    pallas_call x1, Pallas kernels, shards(): pl.pallas_call(local_kernel, in_specs=[whole_in] * 5, out_specs=whole_in,...  2.06 us
    dot_general x1, matrix products, shards(): jnp.dot(gated, out_weight, preferred_element_type=f32).astype(jnp.bfloat16)  1.7 us
  transfers between devices with their start and end apart: 1, of which 1 were waited for; matrix products, arithmetic and copies ran while one was open for 0% of the time, Pallas kernels for 3%

profile of v3, /device:TPU:2, one launch (start us, length us, event | category | flops | bytes accessed | tf_op | source)
XLA Modules:
  0.0 73.9 jit_solution(1020820923619577650)
XLA Ops:
  0.0 0.0 copy-start
  0.0 2.9 %block_state.1 = bf16[32,32,256]{2,1,0:T(8,128)(2,1)} custom-call(bf16[3,256,256]{2,1,0:T(8,128)(2,1)} %bitcast.3, f32[3,3,256]{2,1,0:T(4,128)} %taps_ref.1, f32[16,16]{1,0:T(8,128)} %rates_ref.1), custom_call_target="tpu_custom_call" | custom-call | tf_op jit(solution)/shard_map/block_state/pallas_call | solution.py:290
  2.9 9.5 %all-to-all-start = ((bf16[32,32,256]{2,1,0:T(8,128)(2,1)}), bf16[32,32,256]{2,1,0:T(8,128)(2,1)S(1)}, u32[]{:S(2)}, u32[]{:S(2)}) async-start(bf16[32,32,256]{2,1,0:T(8,128)(2,1)} %block_state.1), calls=%async_computation | async-start | bytes 1048576 | tf_op jit(solution)/shard_map/all_to_all | solution.py:305
  12.4 0.0 copy-start.1
  12.4 1.0 %copy-done.1 = bf16[256,3,256]{2,0,1:T(8,128)(2,1)S(1)} copy-done((bf16[256,3,256]{2,0,1:T(8,128)(2,1)S(1)}, bf16[256,3,256]{2,0,1:T(8,128)(2,1)}, u32[]{:S(2)}) %copy-start.1) | copy-done | bytes 393240
  13.4 0.0 copy-start.2
  13.4 0.7 copy-done.2
  14.1 0.0 copy-start.3
  14.1 0.7 copy-done.3
  14.8 0.0 copy-start.4
  14.8 0.7 copy-done.4
  15.5 0.0 copy-start.5
  15.5 0.7 copy-done.5
  16.2 2.1 %local_conv.1.local_ref = f32[640,256]{1,0:T(8,128)S(1)} custom-call(bf16[3,256,256]{2,1,0:T(8,128)(2,1)S(1)} %bitcast.4, f32[3,3,256]{2,1,0:T(4,128)S(1)} %copy-done.2, f32[16,16]{1,0:T(8,128)S(1)} %copy-done.3, f32[16,16]{1,0:T(8,128)S(1)} %copy-done.4, f32[1,256]{1,0:T(1,128)S(1)} %bitcast.5), custom_call_target="tpu_custom_call" | custom-call | tf_op jit(solution)/shard_map/local_conv/pallas_call | solution.py:306
  18.3 4.8 %all-to-all-done.recv_ref = bf16[32,32,256]{2,1,0:T(8,128)(2,1)S(1)} async-done(((bf16[32,32,256]{2,1,0:T(8,128)(2,1)}), bf16[32,32,256]{2,1,0:T(8,128)(2,1)S(1)}, u32[]{:S(2)}, u32[]{:S(2)}) %all-to-all-start) | async-done | bytes 524320 | tf_op jit(solution)/shard_map/all_to_all | solution.py:305
  23.0 1.0 %carry_gate.1 = f32[256,256]{1,0:T(8,128)S(1)} custom-call(bf16[32,32,256]{2,1,0:T(8,128)(2,1)S(1)} %all-to-all-done.recv_ref, f32[640,256]{1,0:T(8,128)S(1)} %local_conv.1.local_ref), custom_call_target="tpu_custom_call" | custom-call | tf_op jit(solution)/shard_map/carry_gate/pallas_call | solution.py:315
  24.1 48.2 %all-gather.1 = f16[256,4096]{1,0:T(8,128)(2,1)S(1)} all-gather(f16[256,256]{1,0:T(8,128)(2,1)S(1)} %convert_element_type.12), channel_id=1, replica_groups=mesh['ctx'=32,'tp'=16] {'tp'}, dimensions={1}, use_global_device_ids=true | all-gather | bytes 2228224 | tf_op jit(solution)/shard_map/all_gather | solution.py:329
  72.2 0.0 copy-done
  72.2 1.7 %fusion.5 = bf16[256,256]{1,0:T(8,128)(2,1)} fusion(bf16[4096,256]{1,0:T(8,128)(2,1)S(1)} %copy-done, f16[256,4096]{1,0:T(8,128)(2,1)S(1)} %all-gather.1), kind=kOutput, calls=%fused_computation.6 | convolution fusion | flops 544276480 | bytes 4325376 | tf_op jit(solution)/shard_map/dot_general | solution.py:332
  (1 shorter events, 0.0 us)
Async XLA Ops:
  0.0 72.2 %copy-start = (bf16[4096,256]{1,0:T(8,128)(2,1)S(1)}, bf16[4096,256]{1,0:T(8,128)(2,1)}, u32[]{:S(2)}) copy-start(bf16[4096,256]{1,0:T(8,128)(2,1)} %param.11) | copy-start | bytes 6291460
  2.9 20.1 %all-to-all-start = ((bf16[32,32,256]{2,1,0:T(8,128)(2,1)}), bf16[32,32,256]{2,1,0:T(8,128)(2,1)S(1)}, u32[]{:S(2)}, u32[]{:S(2)}) async-start(bf16[32,32,256]{2,1,0:T(8,128)(2,1)} %block_state.1), calls=%async_computation | async-start | bytes 1048576 | tf_op jit(solution)/shard_map/all_to_all | solution.py:305
  12.4 1.0 %copy-start.1 = (bf16[256,3,256]{2,0,1:T(8,128)(2,1)S(1)}, bf16[256,3,256]{2,0,1:T(8,128)(2,1)}, u32[]{:S(2)}) copy-start(bf16[256,3,256]{2,0,1:T(8,128)(2,1)} %param.6) | copy-start | bytes 1179652
  13.4 0.7 copy-start.2
  14.1 0.7 copy-start.3
  14.8 0.7 copy-start.4
  15.5 0.7 copy-start.5

commit v4 on v3

--- a/solution.py
+++ b/solution.py
@@ -9,7 +9,8 @@
 
 SHORT = 3
 CHUNKS = 8
-RIM = 16
+RIM = 8
+EDGE = 16
 LANES = 128
 TABLES = 7
 KERNEL_VMEM = 12 * 2**20
@@ -63,7 +64,7 @@
             visit(i, carry)
         return carry
 
-    return lax.fori_loop(0, steps, step, states, unroll=4)
+    return lax.fori_loop(0, steps, step, states, unroll=8)
 
 
 def chunk_ends(product_ref, ends_ref, lam, rows):
@@ -93,22 +94,23 @@
 
 
 def state_kernel(
-    feat_hbm, taps_hbm, rates_hbm, send_ref,
+    feat_hbm, taps_hbm, rates_hbm, send_ref, edge_ref,
     feat_ref, taps_ref, rates_ref, product_ref, ends_ref, sems,
 ):
     copies = [
         pltpu.make_async_copy(source, target, sems.at[k])
         for k, (source, target) in enumerate(
-            ((feat_hbm, feat_ref), (taps_hbm, taps_ref), (rates_hbm, rates_ref))
+            ((rates_hbm, rates_ref), (taps_hbm, taps_ref), (feat_hbm, feat_ref))
         )
     ]
     for copy in copies:
         copy.start()
-    for copy in copies:
-        copy.wait()
     rows, width = feat_ref.shape[1:]
     modes = rates_ref.shape[0]
+    copies[0].wait()
     lam = per_channel(rates_ref[...], width)
+    copies[1].wait()
+    copies[2].wait()
     save(product_ref, inner_product(feat_ref, taps_ref))
     chunk_ends(product_ref, ends_ref, lam, rows)
     over_chunk = jnp.exp(-lam * float(rows // CHUNKS))
@@ -116,12 +118,13 @@
     for j in range(CHUNKS):
         end = strided(ends_ref, modes * CHUNKS, width, j, modes, CHUNKS)
         total = total * over_chunk + end
-    head = [feat_ref[j, 0:2, :].astype(jnp.float32) for j in (1, 2)]
-    tail = [feat_ref[j, rows - 2 : rows, :].astype(jnp.float32) for j in (1, 2, 0)]
-    own_query = [feat_ref[0, 0:2, :].astype(jnp.float32)]
-    blank = [jnp.zeros((RIM - 12, width), jnp.float32)]
-    rim = jnp.concatenate(head + tail + own_query + blank, 0)
-    block = jnp.concatenate([total, rim], 0).astype(jnp.bfloat16)
+    edges = [
+        feat_ref[j, pl.ds(first, EDGE), :].astype(jnp.float32)[at : at + 2]
+        for first, at in ((0, 0), (rows - EDGE, EDGE - 2))
+        for j in (1, 2)
+    ]
+    block = jnp.concatenate([total] + edges, 0).astype(jnp.bfloat16)
+    edge_ref[...] = feat_ref[0, pl.ds(rows - EDGE, EDGE), :]
     for e in range(send_ref.shape[0]):
         send_ref[e] = block
 
@@ -183,7 +186,7 @@
 
 
 def carry_kernel(
-    recv_ref, local_ref, out_ref,
+    recv_ref, edge_ref, local_ref, out_ref,
     rims_ref, firsts_ref, states_ref, conv_ref,
 ):
     blocks = recv_ref.shape[0]
@@ -201,7 +204,7 @@
     skip = single(3 * SHORT)
 
     for e in range(blocks):
-        edges = recv_ref[e, pl.ds(modes, RIM), :].astype(jnp.float32)
+        edges = recv_ref[e].astype(jnp.float32)[modes : modes + RIM]
         for t in range(width // LANES):
             rims_ref[pl.ds((t * blocks + e) * RIM, RIM), :] = edges[:, t * LANES : (t + 1) * LANES]
 
@@ -219,15 +222,16 @@
         a, b, c = (single(SHORT * j + shift) for shift in range(SHORT))
         return a * zeroth + b * last + c * before_last, a * first + b * zeroth + c * last
 
-    query0, query1 = firsts(0, 10, 8)
     key0, key1 = firsts(1, 0, 4)
     value0, value1 = firsts(2, 2, 6)
     product0, product1 = key0 * value0, key1 * value1
-    for k, array in enumerate((query0, query1, product0, product1)):
+    for k, array in enumerate((product0, product1)):
         firsts_ref[pl.ds(k * blocks, blocks), :] = array
-    own_query0, own_query1, own_product0, own_product1 = (
-        firsts_ref[pl.ds(k * blocks + own, 1), :] for k in range(4)
-    )
+    own_product0, own_product1 = (firsts_ref[pl.ds(k * blocks + own, 1), :] for k in range(2))
+    before = edge_ref[...].astype(jnp.float32)
+    before_last, last = before[EDGE - 2 : EDGE - 1], before[EDGE - 1 : EDGE]
+    own_query0 = local_ref[pl.ds(0, 1), :] + single(1) * last + single(2) * before_last
+    own_query1 = local_ref[pl.ds(1, 1), :] + single(2) * last
 
     state = jnp.zeros((modes, width), jnp.float32)
     for e in range(blocks - 1):
@@ -287,11 +291,14 @@
     by_row = pltpu.VMEM((tiles * rows, LANES), f32)
     by_mode = pltpu.VMEM((tiles * modes * CHUNKS, LANES), f32)
     whole_in = pl.BlockSpec(memory_space=pltpu.VMEM)
-    sent = pl.pallas_call(
+    sent, edge = pl.pallas_call(
         state_kernel,
         in_specs=[pl.BlockSpec(memory_space=pltpu.HBM)] * 3,
-        out_specs=whole_in,
-        out_shape=jax.ShapeDtypeStruct((blocks, modes + RIM, width), jnp.bfloat16),
+        out_specs=(whole_in, whole_in),
+        out_shape=(
+            jax.ShapeDtypeStruct((blocks, modes + RIM, width), jnp.bfloat16),
+            jax.ShapeDtypeStruct((EDGE, width), jnp.bfloat16),
+        ),
         scratch_shapes=[
             pltpu.VMEM(feats.shape, feats.dtype),
             pltpu.VMEM(short_taps.shape, f32),
@@ -303,6 +310,7 @@
         name="block_state",
     )(feats, short_taps, rates)
     received = lax.all_to_all(sent, "ctx", split_axis=0, concat_axis=0, tiled=True)
+    before = lax.ppermute(edge, "ctx", [(i, i + 1) for i in range(blocks - 1)])
     local = pl.pallas_call(
         local_kernel,
         in_specs=[whole_in] * 5,
@@ -314,22 +322,23 @@
     )(feats, short_taps, rates, residues, skip)
     coded = pl.pallas_call(
         carry_kernel,
-        in_specs=[whole_in] * 2,
+        in_specs=[whole_in] * 3,
         out_specs=whole_in,
         out_shape=plane,
         scratch_shapes=[
             pltpu.VMEM((tiles * blocks * RIM, LANES), f32),
-            pltpu.VMEM((4 * blocks, width), f32),
+            pltpu.VMEM((2 * blocks, width), f32),
             by_mode,
             by_row,
         ],
         compiler_params=pltpu.CompilerParams(vmem_limit_bytes=KERNEL_VMEM),
         name="carry_gate",
-    )(received, local)
+    )(received, before, local)
     gathered = lax.all_gather(coded.astype(jnp.float16), "tp", axis=1, tiled=True).astype(f32)
     square = gathered * gathered
-    gated = (square * (gathered * jnp.abs(gathered)) * 2.0**-32).astype(jnp.bfloat16)
-    return jnp.dot(gated, out_weight, preferred_element_type=f32).astype(jnp.bfloat16)
+    gated = (square * (gathered * jnp.abs(gathered))).astype(jnp.bfloat16)
+    mixed = jnp.dot(gated, out_weight, preferred_element_type=f32)
+    return (mixed * 2.0**-32).astype(jnp.bfloat16)
 
 
 def solution(mesh):

time: 74.4 us -> 72.7 us (0.977)
  waiting for transfers between devices: 4.75 us -> 1.47 us
  starting transfers between devices: 9.47 us -> 11.5 us
    all_to_all x1, waiting for transfers between devices: 4.75 us -> 1.46 us  [shards(): lax.all_to_all(sent, 'ctx', split_axis=0, concat_axis=0, tiled=True)]
    ppermute x0 -> x1, starting transfers between devices: none -> 2.06 us  [shards(): before = lax.ppermute(edge, 'ctx', [(i, i + 1) for i in range(blocks - 1)])]
  transfers between devices with their start and end apart: 1 -> 2, of which waited for: 1 -> 1; matrix products, arithmetic and copies ran while one was open for 0% -> 0% of each run, Pallas kernels for 3% -> 3%
where the time goes in v4:
time: 72.7 us; the launch traced here: 72.2 us
  blocking collectives  48.4 us (67%)
  starting transfers between devices  11.5 us (16%)
  Pallas kernels  5.37 us (7%)
  local copies, waits for them, and re-layouts  3.77 us (5%)
  matrix products  1.58 us (2%)
  waiting for transfers between devices  1.47 us (2%)
    all_gather x1, blocking collectives, shards(): lax.all_gather(coded.astype(jnp.float16), 'tp', axis=1, tiled=True)  48.4 us
    all_to_all x1, starting transfers between devices, shards(): lax.all_to_all(sent, 'ctx', split_axis=0, concat_axis=0, tiled=True)  9.46 us
    unnamed x12, local copies, waits for them, and re-layouts  3.77 us
    pallas_call x1, Pallas kernels, shards(): pl.pallas_call(state_kernel, in_specs=[pl.BlockSpec(memory_space=pltpu.HB...  2.56 us
    ppermute x1, starting transfers between devices, shards(): before = lax.ppermute(edge, 'ctx', [(i, i + 1) for i in range(blocks - 1)])  2.06 us
    pallas_call x1, Pallas kernels, shards(): pl.pallas_call(local_kernel, in_specs=[whole_in] * 5, out_specs=whole_in,...  1.87 us
    dot_general x1, matrix products, shards(): mixed = jnp.dot(gated, out_weight, preferred_element_type=f32)  1.58 us
    all_to_all x1, waiting for transfers between devices, shards(): lax.all_to_all(sent, 'ctx', split_axis=0, concat_axis=0, tiled=True)  1.46 us
  transfers between devices with their start and end apart: 2, of which 1 were waited for; matrix products, arithmetic and copies ran while one was open for 0% of the time, Pallas kernels for 3%

profile of v4, /device:TPU:2, one launch (start us, length us, event | category | flops | bytes accessed | tf_op | source)
XLA Modules:
  0.0 72.2 jit_solution(5529148552315472349)
XLA Ops:
  0.0 0.0 copy-start
  0.0 2.6 %block_state.1 = (bf16[32,24,256]{2,1,0:T(8,128)(2,1)}, bf16[16,256]{1,0:T(8,128)(2,1)}) custom-call(bf16[3,256,256]{2,1,0:T(8,128)(2,1)} %bitcast.3, f32[3,3,256]{2,1,0:T(4,128)} %taps_ref.1, f32[16,16]{1,0:T(8,128)} %rates_ref.1), custom_call_target="tpu_custom_call" | custom-call | tf_op jit(solution)/shard_map/block_state/pallas_call | solution.py:294
  2.6 9.5 %all-to-all-start = ((bf16[32,24,256]{2,1,0:T(8,128)(2,1)}), bf16[32,24,256]{2,1,0:T(8,128)(2,1)S(1)}, u32[]{:S(2)}, u32[]{:S(2)}) async-start(bf16[32,24,256]{2,1,0:T(8,128)(2,1)} %get-tuple-element.7), calls=%async_computation | async-start | bytes 786432 | tf_op jit(solution)/shard_map/all_to_all | solution.py:312
  12.0 2.1 %collective-permute-start = (bf16[16,256]{1,0:T(8,128)(2,1)}, bf16[16,256]{1,0:T(8,128)(2,1)S(1)}, u32[]{:S(2)}, u32[]{:S(2)}) collective-permute-start(bf16[16,256]{1,0:T(8,128)(2,1)} %get-tuple-element.8), channel_id=1, source_target_pairs={{0,16},{16,32},{32,48},{48,64},{64,80},{80,96},{96,112},{112,128},... | collective-permute-start | bytes 24584 | tf_op jit(solution)/shard_map/ppermute | solution.py:313
  14.1 0.0 copy-start.1
  14.1 1.0 %copy-done.1 = bf16[256,3,256]{2,0,1:T(8,128)(2,1)S(1)} copy-done((bf16[256,3,256]{2,0,1:T(8,128)(2,1)S(1)}, bf16[256,3,256]{2,0,1:T(8,128)(2,1)}, u32[]{:S(2)}) %copy-start.1) | copy-done | bytes 393240
  15.1 0.0 copy-start.2
  15.1 0.7 copy-done.2
  15.8 0.0 copy-start.3
  15.8 0.7 copy-done.3
  16.5 0.0 copy-start.4
  16.5 0.7 copy-done.4
  17.2 0.0 copy-start.5
  17.2 0.7 copy-done.5
  17.9 1.9 %local_conv.1.local_ref = f32[640,256]{1,0:T(8,128)S(1)} custom-call(bf16[3,256,256]{2,1,0:T(8,128)(2,1)S(1)} %bitcast.4, f32[3,3,256]{2,1,0:T(4,128)S(1)} %copy-done.2, f32[16,16]{1,0:T(8,128)S(1)} %copy-done.3, f32[16,16]{1,0:T(8,128)S(1)} %copy-done.4, f32[1,256]{1,0:T(1,128)S(1)} %bitcast.5), custom_call_target="tpu_custom_call" | custom-call | tf_op jit(solution)/shard_map/local_conv/pallas_call | solution.py:314
  19.8 0.0 collective-permute-done.edge_ref
  19.8 1.5 %all-to-all-done.recv_ref = bf16[32,24,256]{2,1,0:T(8,128)(2,1)S(1)} async-done(((bf16[32,24,256]{2,1,0:T(8,128)(2,1)}), bf16[32,24,256]{2,1,0:T(8,128)(2,1)S(1)}, u32[]{:S(2)}, u32[]{:S(2)}) %all-to-all-start) | async-done | bytes 393248 | tf_op jit(solution)/shard_map/all_to_all | solution.py:312
  21.2 0.9 %carry_gate.1 = f32[256,256]{1,0:T(8,128)S(1)} custom-call(bf16[32,24,256]{2,1,0:T(8,128)(2,1)S(1)} %all-to-all-done.recv_ref, bf16[16,256]{1,0:T(8,128)(2,1)S(1)} %collective-permute-done.edge_ref, f32[640,256]{1,0:T(8,128)S(1)} %local_conv.1.local_ref), custom_call_target="tpu_custom_call" | custom-call | tf_op jit(solution)/shard_map/carry_gate/pallas_call | solution.py:323
  22.2 48.4 %all-gather.1 = f16[256,4096]{1,0:T(8,128)(2,1)S(1)} all-gather(f16[256,256]{1,0:T(8,128)(2,1)S(1)} %convert_element_type.12), channel_id=1, replica_groups=mesh['ctx'=32,'tp'=16] {'tp'}, dimensions={1}, use_global_device_ids=true | all-gather | bytes 2228224 | tf_op jit(solution)/shard_map/all_gather | solution.py:337
  70.6 0.0 copy-done
  70.6 1.6 %fusion.7 = bf16[256,256]{1,0:T(8,128)(2,1)} fusion(bf16[4096,256]{1,0:T(8,128)(2,1)S(1)} %copy-done, f16[256,4096]{1,0:T(8,128)(2,1)S(1)} %all-gather.1), kind=kOutput, calls=%fused_computation.6 | convolution fusion | flops 543293440 | bytes 4325376 | tf_op jit(solution)/shard_map/dot_general | solution.py:340
  (1 shorter events, 0.0 us)
Async XLA Ops:
  0.0 70.6 %copy-start = (bf16[4096,256]{1,0:T(8,128)(2,1)S(1)}, bf16[4096,256]{1,0:T(8,128)(2,1)}, u32[]{:S(2)}) copy-start(bf16[4096,256]{1,0:T(8,128)(2,1)} %param.11) | copy-start | bytes 6291460
  2.6 18.7 %all-to-all-start = ((bf16[32,24,256]{2,1,0:T(8,128)(2,1)}), bf16[32,24,256]{2,1,0:T(8,128)(2,1)S(1)}, u32[]{:S(2)}, u32[]{:S(2)}) async-start(bf16[32,24,256]{2,1,0:T(8,128)(2,1)} %get-tuple-element.7), calls=%async_computation | async-start | bytes 786432 | tf_op jit(solution)/shard_map/all_to_all | solution.py:312
  12.0 7.7 %collective-permute-start = (bf16[16,256]{1,0:T(8,128)(2,1)}, bf16[16,256]{1,0:T(8,128)(2,1)S(1)}, u32[]{:S(2)}, u32[]{:S(2)}) collective-permute-start(bf16[16,256]{1,0:T(8,128)(2,1)} %get-tuple-element.8), channel_id=1, source_target_pairs={{0,16},{16,32},{32,48},{48,64},{64,80},{80,96},{96,112},{112,128},... | collective-permute-start | bytes 24584 | tf_op jit(solution)/shard_map/ppermute | solution.py:313
  14.1 1.0 %copy-start.1 = (bf16[256,3,256]{2,0,1:T(8,128)(2,1)S(1)}, bf16[256,3,256]{2,0,1:T(8,128)(2,1)}, u32[]{:S(2)}) copy-start(bf16[256,3,256]{2,0,1:T(8,128)(2,1)} %param.6) | copy-start | bytes 1179652
  15.1 0.7 copy-start.2
  15.8 0.7 copy-start.3
  16.5 0.7 copy-start.4
  17.2 0.7 copy-start.5

commit v5 on v4

--- a/solution.py
+++ b/solution.py
@@ -64,12 +64,11 @@
             visit(i, carry)
         return carry
 
-    return lax.fori_loop(0, steps, step, states, unroll=8)
-
-
-def chunk_ends(product_ref, ends_ref, lam, rows):
-    modes, width = lam.shape
-    decay = jnp.exp(-lam)
+    return lax.fori_loop(0, steps, step, states, unroll=16)
+
+
+def chunk_ends(product_ref, ends_ref, decay, rows):
+    modes, width = decay.shape
     for t in range(width // LANES):
         blank = tuple(jnp.zeros((CHUNKS, LANES), jnp.float32) for _ in range(modes))
         part = [spread(decay, r, t) for r in range(modes)]
@@ -78,15 +77,25 @@
             ends_ref[pl.ds((t * modes + r) * CHUNKS, CHUNKS), :] = end
 
 
-def channel_taps(taps_ref, j):
-    return [taps_ref[s, j : j + 1, :] for s in range(SHORT)]
-
-
-def inner_product(feat_ref, taps_ref):
+def table(tables_ref, modes, k):
+    return tables_ref[pl.ds(k * modes, modes), :]
+
+
+def single(tables_ref, modes, k):
+    return tables_ref[pl.ds(TABLES * modes + k, 1), :]
+
+
+def channel_taps(tables_ref, modes, j):
+    return [single(tables_ref, modes, SHORT * j + shift) for shift in range(SHORT)]
+
+
+def inner_product(feat_ref, tables_ref, modes):
     rows, width = feat_ref.shape[1:]
     zero = jnp.zeros((1, width), jnp.float32)
     keys, values = (
-        short_filter(feat_ref[j].astype(jnp.float32), channel_taps(taps_ref, j), zero, zero)
+        short_filter(
+            feat_ref[j].astype(jnp.float32), channel_taps(tables_ref, modes, j), zero, zero
+        )
         for j in (1, 2)
     )
     row = lax.broadcasted_iota(jnp.int32, (rows, width), 0)
@@ -94,26 +103,52 @@
 
 
 def state_kernel(
-    feat_hbm, taps_hbm, rates_hbm, send_ref, edge_ref,
-    feat_ref, taps_ref, rates_ref, product_ref, ends_ref, sems,
+    feat_hbm, taps_hbm, rates_hbm, residues_hbm, skip_hbm, send_ref, edge_ref, tables_ref,
+    feat_ref, taps_ref, rates_ref, residues_ref, skip_ref, product_ref, ends_ref, sems,
 ):
     copies = [
         pltpu.make_async_copy(source, target, sems.at[k])
         for k, (source, target) in enumerate(
-            ((rates_hbm, rates_ref), (taps_hbm, taps_ref), (feat_hbm, feat_ref))
+            (
+                (rates_hbm, rates_ref), (residues_hbm, residues_ref), (taps_hbm, taps_ref),
+                (skip_hbm, skip_ref), (feat_hbm, feat_ref),
+            )
         )
     ]
     for copy in copies:
         copy.start()
     rows, width = feat_ref.shape[1:]
     modes = rates_ref.shape[0]
+    steps = rows // CHUNKS
     copies[0].wait()
-    lam = per_channel(rates_ref[...], width)
     copies[1].wait()
+    rates = rates_ref[...]
+    lam = per_channel(rates, width)
+    decay = jnp.exp(-lam)
+    over_chunk = jnp.exp(-lam * float(steps))
+    coef = per_channel(residues_ref[...] * jnp.sqrt(2.0 * rates), width)
+    for k, values in enumerate(
+        (
+            decay,
+            jnp.exp(lam),
+            jnp.exp(-lam * float(rows - 2)),
+            jnp.exp(-lam * float(rows - 1)),
+            jnp.exp(-lam * float(rows)),
+            over_chunk,
+            coef,
+        )
+    ):
+        tables_ref[pl.ds(k * modes, modes), :] = values
     copies[2].wait()
-    save(product_ref, inner_product(feat_ref, taps_ref))
-    chunk_ends(product_ref, ends_ref, lam, rows)
-    over_chunk = jnp.exp(-lam * float(rows // CHUNKS))
+    copies[3].wait()
+    taps = [taps_ref[shift, j : j + 1, :] for j in range(3) for shift in range(SHORT)]
+    unused = [jnp.zeros((modes - 3 * SHORT - 1, width), jnp.float32)]
+    tables_ref[pl.ds(TABLES * modes, modes), :] = jnp.concatenate(
+        taps + [skip_ref[...]] + unused, 0
+    )
+    copies[4].wait()
+    save(product_ref, inner_product(feat_ref, tables_ref, modes))
+    chunk_ends(product_ref, ends_ref, decay, rows)
     total = jnp.zeros((modes, width), jnp.float32)
     for j in range(CHUNKS):
         end = strided(ends_ref, modes * CHUNKS, width, j, modes, CHUNKS)
@@ -123,27 +158,28 @@
         for first, at in ((0, 0), (rows - EDGE, EDGE - 2))
         for j in (1, 2)
     ]
-    block = jnp.concatenate([total] + edges, 0).astype(jnp.bfloat16)
+    edges = jnp.concatenate(edges, 0)
+    block = jnp.concatenate(
+        [a[:, t * LANES : (t + 1) * LANES] for a in (total, edges) for t in range(width // LANES)], 0
+    )
+    block = block.astype(jnp.bfloat16)
     edge_ref[...] = feat_ref[0, pl.ds(rows - EDGE, EDGE), :]
     for e in range(send_ref.shape[0]):
         send_ref[e] = block
 
 
-def local_kernel(
-    feat_ref, taps_ref, rates_ref, residues_ref, skip_ref, local_ref,
-    product_ref, states_ref, conv_ref,
-):
+def local_kernel(feat_ref, tables_ref, local_ref, product_ref, states_ref, conv_ref):
     rows, width = feat_ref.shape[1:]
-    modes = rates_ref.shape[0]
+    modes = tables_ref.shape[0] // (TABLES + 1)
     steps = rows // CHUNKS
-    lam = per_channel(rates_ref[...], width)
-    coef = per_channel(residues_ref[...] * jnp.sqrt(2.0 * rates_ref[...]), width)
+    decay, over_chunk, coef = (table(tables_ref, modes, k) for k in (0, 5, 6))
     zero = jnp.zeros((1, width), jnp.float32)
-    query = short_filter(feat_ref[0].astype(jnp.float32), channel_taps(taps_ref, 0), zero, zero)
-    product = inner_product(feat_ref, taps_ref)
+    query = short_filter(
+        feat_ref[0].astype(jnp.float32), channel_taps(tables_ref, modes, 0), zero, zero
+    )
+    product = inner_product(feat_ref, tables_ref, modes)
     save(product_ref, product)
-    chunk_ends(product_ref, states_ref, lam, rows)
-    over_chunk = jnp.exp(-lam * float(steps))
+    chunk_ends(product_ref, states_ref, decay, rows)
     state = jnp.zeros((modes, width), jnp.float32)
     for j in range(CHUNKS):
         end = strided(states_ref, modes * CHUNKS, width, j, modes, CHUNKS)
@@ -151,7 +187,6 @@
             where = pl.ds(t * modes * CHUNKS + j, modes, stride=CHUNKS)
             states_ref[where, :] = state[:, t * LANES : (t + 1) * LANES]
         state = state * over_chunk + end
-    decay = jnp.exp(-lam)
     for t in range(width // LANES):
         part = [spread(decay, r, t) for r in range(modes)]
         scale = [spread(coef, r, t) for r in range(modes)]
@@ -164,25 +199,10 @@
             conv_ref[pl.ds(t * rows + i, CHUNKS, stride=steps), :] = total
 
         recur(product_ref, t * rows, part, begin, steps, visit)
-    for k, table in enumerate(
-        (
-            decay,
-            jnp.exp(lam),
-            jnp.exp(-lam * float(rows - 2)),
-            jnp.exp(-lam * float(rows - 1)),
-            jnp.exp(-lam * float(rows)),
-            over_chunk,
-            coef,
-        )
-    ):
-        local_ref[pl.ds(2 * rows + k * modes, modes), :] = table
-    singles = 2 * rows + TABLES * modes
-    for j in range(3):
-        for shift, tap in enumerate(channel_taps(taps_ref, j)):
-            local_ref[pl.ds(singles + SHORT * j + shift, 1), :] = tap
-    local_ref[pl.ds(singles + 3 * SHORT, 1), :] = skip_ref[...]
+    skip = single(tables_ref, modes, 3 * SHORT)
+    local_ref[pl.ds(2 * rows, (TABLES + 1) * modes), :] = tables_ref[...]
     local_ref[pl.ds(0, rows), :] = query
-    local_ref[pl.ds(rows, rows), :] = query * (whole(conv_ref, rows, width) + skip_ref[...] * product)
+    local_ref[pl.ds(rows, rows), :] = query * (whole(conv_ref, rows, width) + skip * product)
 
 
 def carry_kernel(
@@ -191,25 +211,22 @@
 ):
     blocks = recv_ref.shape[0]
     rows, width = out_ref.shape
-    modes = recv_ref.shape[1] - RIM
+    tiles = width // LANES
+    modes = recv_ref.shape[1] // tiles - RIM
     steps = rows // CHUNKS
     own = lax.axis_index("ctx")
+    tables_ref = local_ref.at[pl.ds(2 * rows, (TABLES + 1) * modes)]
     decay, grow, weight1, weight0, over_block, over_chunk, coef = (
-        local_ref[pl.ds(2 * rows + k * modes, modes), :] for k in range(TABLES)
-    )
-
-    def single(k):
-        return local_ref[pl.ds(2 * rows + TABLES * modes + k, 1), :]
-
-    skip = single(3 * SHORT)
+        table(tables_ref, modes, k) for k in range(TABLES)
+    )
+    skip = single(tables_ref, modes, 3 * SHORT)
 
     for e in range(blocks):
-        edges = recv_ref[e].astype(jnp.float32)[modes : modes + RIM]
-        for t in range(width // LANES):
-            rims_ref[pl.ds((t * blocks + e) * RIM, RIM), :] = edges[:, t * LANES : (t + 1) * LANES]
+        edges = recv_ref[e, pl.ds(tiles * modes, tiles * RIM), :].astype(jnp.float32)
+        rims_ref[pl.ds(e * tiles * RIM, tiles * RIM), :] = edges
 
     def edge(k):
-        return strided(rims_ref, blocks * RIM, width, k, blocks, RIM)
+        return strided(rims_ref, RIM, width, k, blocks, tiles * RIM)
 
     block_row = lax.broadcasted_iota(jnp.int32, (blocks, width), 0)
 
@@ -219,7 +236,7 @@
     def firsts(j, head, tail):
         zeroth, first = edge(head), edge(head + 1)
         before_last, last = earlier(tail), earlier(tail + 1)
-        a, b, c = (single(SHORT * j + shift) for shift in range(SHORT))
+        a, b, c = channel_taps(tables_ref, modes, j)
         return a * zeroth + b * last + c * before_last, a * first + b * zeroth + c * last
 
     key0, key1 = firsts(1, 0, 4)
@@ -230,13 +247,15 @@
     own_product0, own_product1 = (firsts_ref[pl.ds(k * blocks + own, 1), :] for k in range(2))
     before = edge_ref[...].astype(jnp.float32)
     before_last, last = before[EDGE - 2 : EDGE - 1], before[EDGE - 1 : EDGE]
-    own_query0 = local_ref[pl.ds(0, 1), :] + single(1) * last + single(2) * before_last
-    own_query1 = local_ref[pl.ds(1, 1), :] + single(2) * last
+    _, b, c = channel_taps(tables_ref, modes, 0)
+    own_query0 = local_ref[pl.ds(0, 1), :] + b * last + c * before_last
+    own_query1 = local_ref[pl.ds(1, 1), :] + c * last
 
     state = jnp.zeros((modes, width), jnp.float32)
     for e in range(blocks - 1):
+        end = [recv_ref[e, pl.ds(t * modes, modes), :].astype(jnp.float32) for t in range(tiles)]
         added = (
-            recv_ref[e, pl.ds(0, modes), :].astype(jnp.float32)
+            jnp.concatenate(end, 1)
             + weight0 * product0[e : e + 1]
             + weight1 * product1[e : e + 1]
         )
@@ -287,39 +306,43 @@
     skip = skip.reshape(1, width)
     f32 = jnp.float32
     tiles = width // LANES
+    payload = tiles * (modes + RIM)
     plane = jax.ShapeDtypeStruct((rows, width), f32)
     by_row = pltpu.VMEM((tiles * rows, LANES), f32)
     by_mode = pltpu.VMEM((tiles * modes * CHUNKS, LANES), f32)
     whole_in = pl.BlockSpec(memory_space=pltpu.VMEM)
-    sent, edge = pl.pallas_call(
+    sent, edge, tables = pl.pallas_call(
         state_kernel,
-        in_specs=[pl.BlockSpec(memory_space=pltpu.HBM)] * 3,
-        out_specs=(whole_in, whole_in),
+        in_specs=[pl.BlockSpec(memory_space=pltpu.HBM)] * 5,
+        out_specs=(whole_in,) * 3,
         out_shape=(
-            jax.ShapeDtypeStruct((blocks, modes + RIM, width), jnp.bfloat16),
+            jax.ShapeDtypeStruct((blocks, payload, LANES), jnp.bfloat16),
             jax.ShapeDtypeStruct((EDGE, width), jnp.bfloat16),
+            jax.ShapeDtypeStruct(((TABLES + 1) * modes, width), f32),
         ),
         scratch_shapes=[
             pltpu.VMEM(feats.shape, feats.dtype),
             pltpu.VMEM(short_taps.shape, f32),
             pltpu.VMEM(rates.shape, f32),
+            pltpu.VMEM(residues.shape, f32),
+            pltpu.VMEM(skip.shape, f32),
             by_row,
             by_mode,
-            pltpu.SemaphoreType.DMA((3,)),
+            pltpu.SemaphoreType.DMA((5,)),
         ],
         name="block_state",
-    )(feats, short_taps, rates)
+    )(feats, short_taps, rates, residues, skip)
     received = lax.all_to_all(sent, "ctx", split_axis=0, concat_axis=0, tiled=True)
     before = lax.ppermute(edge, "ctx", [(i, i + 1) for i in range(blocks - 1)])
     local = pl.pallas_call(
         local_kernel,
-        in_specs=[whole_in] * 5,
+        in_specs=[whole_in] * 2,
         out_specs=whole_in,
         out_shape=jax.ShapeDtypeStruct((2 * rows + (TABLES + 1) * modes, width), f32),
         scratch_shapes=[by_row, by_mode, by_row],
         compiler_params=pltpu.CompilerParams(vmem_limit_bytes=KERNEL_VMEM),
         name="local_conv",
-    )(feats, short_taps, rates, residues, skip)
+    )(feats, tables)
     coded = pl.pallas_call(
         carry_kernel,
         in_specs=[whole_in] * 3,

time: 72.7 us -> 72.6 us (level)
  waiting for transfers between devices: 1.47 us -> 3.74 us
  local copies, waits for them, and re-layouts: 3.77 us -> 1.9 us
    all_to_all x1, waiting for transfers between devices: 1.46 us -> 3.67 us  [shards(): lax.all_to_all(sent, 'ctx', split_axis=0, concat_axis=0, tiled=True)]
    unnamed x12 -> x6, local copies, waits for them, and re-layouts: 3.77 us -> 1.9 us
  transfers between devices with their start and end apart: 2 -> 2, of which waited for: 1 -> 2; matrix products, arithmetic and copies ran while one was open for 0% -> 0% of each run, Pallas kernels for 3% -> 2%
where the time goes in v5:
time: 72.6 us; the launch traced here: 72.3 us
  blocking collectives  48.4 us (67%)
  starting transfers between devices  11.5 us (16%)
  Pallas kernels  5.05 us (7%)
  waiting for transfers between devices  3.74 us (5%)
  local copies, waits for them, and re-layouts  1.9 us (3%)
  matrix products  1.58 us (2%)
    all_gather x1, blocking collectives, shards(): lax.all_gather(coded.astype(jnp.float16), 'tp', axis=1, tiled=True)  48.4 us
    all_to_all x1, starting transfers between devices, shards(): lax.all_to_all(sent, 'ctx', split_axis=0, concat_axis=0, tiled=True)  9.46 us
    all_to_all x1, waiting for transfers between devices, shards(): lax.all_to_all(sent, 'ctx', split_axis=0, concat_axis=0, tiled=True)  3.67 us
    pallas_call x1, Pallas kernels, shards(): pl.pallas_call(state_kernel, in_specs=[pl.BlockSpec(memory_space=pltpu.HB...  2.6 us
    ppermute x1, starting transfers between devices, shards(): before = lax.ppermute(edge, 'ctx', [(i, i + 1) for i in range(blocks - 1)])  2.06 us
    unnamed x6, local copies, waits for them, and re-layouts  1.9 us
    dot_general x1, matrix products, shards(): mixed = jnp.dot(gated, out_weight, preferred_element_type=f32)  1.58 us
    pallas_call x1, Pallas kernels, shards(): pl.pallas_call(local_kernel, in_specs=[whole_in] * 2, out_specs=whole_in,...  1.48 us
  transfers between devices with their start and end apart: 2, of which 2 were waited for; matrix products, arithmetic and copies ran while one was open for 0% of the time, Pallas kernels for 2%

profile of v5, /device:TPU:2, one launch (start us, length us, event | category | flops | bytes accessed | tf_op | source)
XLA Modules:
  0.0 72.3 jit_solution(2968767734636504759)
XLA Ops:
  0.0 0.0 copy-start
  0.0 2.6 %block_state.1 = (bf16[32,48,128]{2,1,0:T(8,128)(2,1)}, bf16[16,256]{1,0:T(8,128)(2,1)}, f32[128,256]{1,0:T(8,128)}) custom-call(bf16[3,256,256]{2,1,0:T(8,128)(2,1)} %bitcast.3, f32[3,3,256]{2,1,0:T(4,128)} %taps_hbm.1, f32[16,16]{1,0:T(8,128)} %rates_hbm.1, f32[16,16]{1,0:T(8,128)} %residues_hbm.1, f32[1,256]{1,0:T(1,128)} %bitcast.5), custom_call_target="tpu_custom_call" | custom-call | tf_op jit(solution)/shard_map/block_state/pallas_call | solution.py:314
  2.6 9.5 %all-to-all-start = ((bf16[32,48,128]{2,1,0:T(8,128)(2,1)}), bf16[32,48,128]{2,1,0:T(8,128)(2,1)S(1)}, u32[]{:S(2)}, u32[]{:S(2)}) async-start(bf16[32,48,128]{2,1,0:T(8,128)(2,1)} %get-tuple-element.8), calls=%async_computation | async-start | bytes 786432 | tf_op jit(solution)/shard_map/all_to_all | solution.py:335
  12.1 2.1 %collective-permute-start = (bf16[16,256]{1,0:T(8,128)(2,1)}, bf16[16,256]{1,0:T(8,128)(2,1)S(1)}, u32[]{:S(2)}, u32[]{:S(2)}) collective-permute-start(bf16[16,256]{1,0:T(8,128)(2,1)} %get-tuple-element.9), channel_id=1, source_target_pairs={{0,16},{16,32},{32,48},{48,64},{64,80},{80,96},{96,112},{112,128},... | collective-permute-start | bytes 24584 | tf_op jit(solution)/shard_map/ppermute | solution.py:336
  14.1 0.0 copy-start.1
  14.2 1.0 %copy-done.1 = bf16[256,3,256]{2,0,1:T(8,128)(2,1)S(1)} copy-done((bf16[256,3,256]{2,0,1:T(8,128)(2,1)S(1)}, bf16[256,3,256]{2,0,1:T(8,128)(2,1)}, u32[]{:S(2)}) %copy-start.1) | copy-done | bytes 393240
  15.1 0.0 copy-start.2
  15.1 0.9 %copy-done.2 = f32[128,256]{1,0:T(8,128)S(1)} copy-done((f32[128,256]{1,0:T(8,128)S(1)}, f32[128,256]{1,0:T(8,128)}, u32[]{:S(2)}) %copy-start.2) | copy-done | bytes 131096
  16.0 1.5 %local_conv.1.local_ref = f32[640,256]{1,0:T(8,128)S(1)} custom-call(bf16[3,256,256]{2,1,0:T(8,128)(2,1)S(1)} %bitcast.4, f32[128,256]{1,0:T(8,128)S(1)} %copy-done.2), custom_call_target="tpu_custom_call" | custom-call | tf_op jit(solution)/shard_map/local_conv/pallas_call | solution.py:337
  17.5 0.1 collective-permute-done.edge_ref
  17.6 3.7 %all-to-all-done.recv_ref = bf16[32,48,128]{2,1,0:T(8,128)(2,1)S(1)} async-done(((bf16[32,48,128]{2,1,0:T(8,128)(2,1)}), bf16[32,48,128]{2,1,0:T(8,128)(2,1)S(1)}, u32[]{:S(2)}, u32[]{:S(2)}) %all-to-all-start) | async-done | bytes 393248 | tf_op jit(solution)/shard_map/all_to_all | solution.py:335
  21.3 1.0 %carry_gate.1 = f32[256,256]{1,0:T(8,128)S(1)} custom-call(bf16[32,48,128]{2,1,0:T(8,128)(2,1)S(1)} %all-to-all-done.recv_ref, bf16[16,256]{1,0:T(8,128)(2,1)S(1)} %collective-permute-done.edge_ref, f32[640,256]{1,0:T(8,128)S(1)} %local_conv.1.local_ref), custom_call_target="tpu_custom_call" | custom-call | tf_op jit(solution)/shard_map/carry_gate/pallas_call | solution.py:346
  22.3 48.4 %all-gather.1 = f16[256,4096]{1,0:T(8,128)(2,1)S(1)} all-gather(f16[256,256]{1,0:T(8,128)(2,1)S(1)} %convert_element_type.12), channel_id=1, replica_groups=mesh['ctx'=32,'tp'=16] {'tp'}, dimensions={1}, use_global_device_ids=true | all-gather | bytes 2228224 | tf_op jit(solution)/shard_map/all_gather | solution.py:360
  70.7 0.0 copy-done
  70.7 1.6 %fusion.7 = bf16[256,256]{1,0:T(8,128)(2,1)} fusion(bf16[4096,256]{1,0:T(8,128)(2,1)S(1)} %copy-done, f16[256,4096]{1,0:T(8,128)(2,1)S(1)} %all-gather.1), kind=kOutput, calls=%fused_computation.6 | convolution fusion | flops 543293440 | bytes 4325376 | tf_op jit(solution)/shard_map/dot_general | solution.py:363
  (1 shorter events, 0.0 us)
Async XLA Ops:
  0.0 70.7 %copy-start = (bf16[4096,256]{1,0:T(8,128)(2,1)S(1)}, bf16[4096,256]{1,0:T(8,128)(2,1)}, u32[]{:S(2)}) copy-start(bf16[4096,256]{1,0:T(8,128)(2,1)} %param.11) | copy-start | bytes 6291460
  2.6 18.7 %all-to-all-start = ((bf16[32,48,128]{2,1,0:T(8,128)(2,1)}), bf16[32,48,128]{2,1,0:T(8,128)(2,1)S(1)}, u32[]{:S(2)}, u32[]{:S(2)}) async-start(bf16[32,48,128]{2,1,0:T(8,128)(2,1)} %get-tuple-element.8), calls=%async_computation | async-start | bytes 786432 | tf_op jit(solution)/shard_map/all_to_all | solution.py:335
  12.1 5.5 %collective-permute-start = (bf16[16,256]{1,0:T(8,128)(2,1)}, bf16[16,256]{1,0:T(8,128)(2,1)S(1)}, u32[]{:S(2)}, u32[]{:S(2)}) collective-permute-start(bf16[16,256]{1,0:T(8,128)(2,1)} %get-tuple-element.9), channel_id=1, source_target_pairs={{0,16},{16,32},{32,48},{48,64},{64,80},{80,96},{96,112},{112,128},... | collective-permute-start | bytes 24584 | tf_op jit(solution)/shard_map/ppermute | solution.py:336
  14.1 1.0 %copy-start.1 = (bf16[256,3,256]{2,0,1:T(8,128)(2,1)S(1)}, bf16[256,3,256]{2,0,1:T(8,128)(2,1)}, u32[]{:S(2)}) copy-start(bf16[256,3,256]{2,0,1:T(8,128)(2,1)} %param.6) | copy-start | bytes 1179652
  15.1 0.9 %copy-start.2 = (f32[128,256]{1,0:T(8,128)S(1)}, f32[128,256]{1,0:T(8,128)}, u32[]{:S(2)}) copy-start(f32[128,256]{1,0:T(8,128)} %get-tuple-element.10.tables_ref) | copy-start | bytes 393220

commit v6 on v5

--- a/solution.py
+++ b/solution.py
@@ -318,7 +318,7 @@
         out_shape=(
             jax.ShapeDtypeStruct((blocks, payload, LANES), jnp.bfloat16),
             jax.ShapeDtypeStruct((EDGE, width), jnp.bfloat16),
-            jax.ShapeDtypeStruct(((TABLES + 1) * modes, width), f32),
+            pltpu.VMEM(((TABLES + 1) * modes, width), f32),
         ),
         scratch_shapes=[
             pltpu.VMEM(feats.shape, feats.dtype),

time: 72.6 us -> 72.5 us (level)
  waiting for transfers between devices: 3.74 us -> 4.65 us
  local copies, waits for them, and re-layouts: 1.9 us -> 1 us
    ppermute x1, waiting for transfers between devices: 0.07 us -> 0.97 us  [shards(): before = lax.ppermute(edge, 'ctx', [(i, i + 1) for i in range(blocks - 1)])]
    unnamed x6 -> x4, local copies, waits for them, and re-layouts: 1.9 us -> 1 us
where the time goes in v6:
time: 72.5 us; the launch traced here: 72.3 us
  blocking collectives  48.4 us (67%)
  starting transfers between devices  11.5 us (16%)
  Pallas kernels  5.03 us (7%)
  waiting for transfers between devices  4.65 us (6%)
  matrix products  1.58 us (2%)
  local copies, waits for them, and re-layouts  1 us (1%)
    all_gather x1, blocking collectives, shards(): lax.all_gather(coded.astype(jnp.float16), 'tp', axis=1, tiled=True)  48.4 us
    all_to_all x1, starting transfers between devices, shards(): lax.all_to_all(sent, 'ctx', split_axis=0, concat_axis=0, tiled=True)  9.46 us
    all_to_all x1, waiting for transfers between devices, shards(): lax.all_to_all(sent, 'ctx', split_axis=0, concat_axis=0, tiled=True)  3.67 us
    pallas_call x1, Pallas kernels, shards(): pl.pallas_call(state_kernel, in_specs=[pl.BlockSpec(memory_space=pltpu.HB...  2.58 us
    ppermute x1, starting transfers between devices, shards(): before = lax.ppermute(edge, 'ctx', [(i, i + 1) for i in range(blocks - 1)])  2.06 us
    dot_general x1, matrix products, shards(): mixed = jnp.dot(gated, out_weight, preferred_element_type=f32)  1.58 us
    pallas_call x1, Pallas kernels, shards(): pl.pallas_call(local_kernel, in_specs=[whole_in] * 2, out_specs=whole_in,...  1.48 us
  transfers between devices with their start and end apart: 2, of which 2 were waited for; matrix products, arithmetic and copies ran while one was open for 0% of the time, Pallas kernels for 2%

profile of v6, /device:TPU:2, one launch (start us, length us, event | category | flops | bytes accessed | tf_op | source)
XLA Modules:
  0.0 72.3 jit_solution(18430569123369187383)
XLA Ops:
  0.0 0.0 copy-start
  0.0 2.6 %block_state.1 = (bf16[32,48,128]{2,1,0:T(8,128)(2,1)}, bf16[16,256]{1,0:T(8,128)(2,1)}, f32[128,256]{1,0:T(8,128)S(1)}) custom-call(bf16[3,256,256]{2,1,0:T(8,128)(2,1)} %bitcast.3, f32[3,3,256]{2,1,0:T(4,128)} %taps_hbm.1, f32[16,16]{1,0:T(8,128)} %rates_hbm.1, f32[16,16]{1,0:T(8,128)} %residues_hbm.1, f32[1,256]{1,0:T(1,128)} %bitcast.5), custom_call_target="tpu_custom_call" | custom-call | tf_op jit(solution)/shard_map/block_state/pallas_call | solution.py:314
  2.6 9.5 %all-to-all-start = ((bf16[32,48,128]{2,1,0:T(8,128)(2,1)}), bf16[32,48,128]{2,1,0:T(8,128)(2,1)S(1)}, u32[]{:S(2)}, u32[]{:S(2)}) async-start(bf16[32,48,128]{2,1,0:T(8,128)(2,1)} %get-tuple-element.8), calls=%async_computation | async-start | bytes 786432 | tf_op jit(solution)/shard_map/all_to_all | solution.py:335
  12.1 2.1 %collective-permute-start = (bf16[16,256]{1,0:T(8,128)(2,1)}, bf16[16,256]{1,0:T(8,128)(2,1)S(1)}, u32[]{:S(2)}, u32[]{:S(2)}) collective-permute-start(bf16[16,256]{1,0:T(8,128)(2,1)} %get-tuple-element.9), channel_id=1, source_target_pairs={{0,16},{16,32},{32,48},{48,64},{64,80},{80,96},{96,112},{112,128},... | collective-permute-start | bytes 24584 | tf_op jit(solution)/shard_map/ppermute | solution.py:336
  14.1 0.0 copy-start.1
  14.1 1.0 %copy-done.1 = bf16[256,3,256]{2,0,1:T(8,128)(2,1)S(1)} copy-done((bf16[256,3,256]{2,0,1:T(8,128)(2,1)S(1)}, bf16[256,3,256]{2,0,1:T(8,128)(2,1)}, u32[]{:S(2)}) %copy-start.1) | copy-done | bytes 393240
  15.1 1.5 %local_conv.1.local_ref = f32[640,256]{1,0:T(8,128)S(1)} custom-call(bf16[3,256,256]{2,1,0:T(8,128)(2,1)S(1)} %bitcast.4, f32[128,256]{1,0:T(8,128)S(1)} %get-tuple-element.10.tables_ref), custom_call_target="tpu_custom_call" | custom-call | tf_op jit(solution)/shard_map/local_conv/pallas_call | solution.py:337
  16.6 1.0 %collective-permute-done.edge_ref = bf16[16,256]{1,0:T(8,128)(2,1)S(1)} collective-permute-done((bf16[16,256]{1,0:T(8,128)(2,1)}, bf16[16,256]{1,0:T(8,128)(2,1)S(1)}, u32[]{:S(2)}, u32[]{:S(2)}) %collective-permute-start) | collective-permute-done | bytes 8224 | tf_op jit(solution)/shard_map/ppermute | solution.py:336
  17.6 3.7 %all-to-all-done.recv_ref = bf16[32,48,128]{2,1,0:T(8,128)(2,1)S(1)} async-done(((bf16[32,48,128]{2,1,0:T(8,128)(2,1)}), bf16[32,48,128]{2,1,0:T(8,128)(2,1)S(1)}, u32[]{:S(2)}, u32[]{:S(2)}) %all-to-all-start) | async-done | bytes 393248 | tf_op jit(solution)/shard_map/all_to_all | solution.py:335
  21.3 1.0 %carry_gate.1 = f32[256,256]{1,0:T(8,128)S(1)} custom-call(bf16[32,48,128]{2,1,0:T(8,128)(2,1)S(1)} %all-to-all-done.recv_ref, bf16[16,256]{1,0:T(8,128)(2,1)S(1)} %collective-permute-done.edge_ref, f32[640,256]{1,0:T(8,128)S(1)} %local_conv.1.local_ref), custom_call_target="tpu_custom_call" | custom-call | tf_op jit(solution)/shard_map/carry_gate/pallas_call | solution.py:346
  22.3 48.4 %all-gather.1 = f16[256,4096]{1,0:T(8,128)(2,1)S(1)} all-gather(f16[256,256]{1,0:T(8,128)(2,1)S(1)} %convert_element_type.12), channel_id=1, replica_groups=mesh['ctx'=32,'tp'=16] {'tp'}, dimensions={1}, use_global_device_ids=true | all-gather | bytes 2228224 | tf_op jit(solution)/shard_map/all_gather | solution.py:360
  70.7 0.0 copy-done
  70.7 1.6 %fusion.7 = bf16[256,256]{1,0:T(8,128)(2,1)} fusion(bf16[4096,256]{1,0:T(8,128)(2,1)S(1)} %copy-done, f16[256,4096]{1,0:T(8,128)(2,1)S(1)} %all-gather.1), kind=kOutput, calls=%fused_computation.6 | convolution fusion | flops 543293440 | bytes 4325376 | tf_op jit(solution)/shard_map/dot_general | solution.py:363
  (1 shorter events, 0.0 us)
Async XLA Ops:
  0.0 70.7 %copy-start = (bf16[4096,256]{1,0:T(8,128)(2,1)S(1)}, bf16[4096,256]{1,0:T(8,128)(2,1)}, u32[]{:S(2)}) copy-start(bf16[4096,256]{1,0:T(8,128)(2,1)} %param.11) | copy-start | bytes 6291460
  2.6 18.7 %all-to-all-start = ((bf16[32,48,128]{2,1,0:T(8,128)(2,1)}), bf16[32,48,128]{2,1,0:T(8,128)(2,1)S(1)}, u32[]{:S(2)}, u32[]{:S(2)}) async-start(bf16[32,48,128]{2,1,0:T(8,128)(2,1)} %get-tuple-element.8), calls=%async_computation | async-start | bytes 786432 | tf_op jit(solution)/shard_map/all_to_all | solution.py:335
  12.1 5.5 %collective-permute-start = (bf16[16,256]{1,0:T(8,128)(2,1)}, bf16[16,256]{1,0:T(8,128)(2,1)S(1)}, u32[]{:S(2)}, u32[]{:S(2)}) collective-permute-start(bf16[16,256]{1,0:T(8,128)(2,1)} %get-tuple-element.9), channel_id=1, source_target_pairs={{0,16},{16,32},{32,48},{48,64},{64,80},{80,96},{96,112},{112,128},... | collective-permute-start | bytes 24584 | tf_op jit(solution)/shard_map/ppermute | solution.py:336
  14.1 1.0 %copy-start.1 = (bf16[256,3,256]{2,0,1:T(8,128)(2,1)S(1)}, bf16[256,3,256]{2,0,1:T(8,128)(2,1)}, u32[]{:S(2)}) copy-start(bf16[256,3,256]{2,0,1:T(8,128)(2,1)} %param.6) | copy-start | bytes 1179652

commit v7 on v6

--- a/solution.py
+++ b/solution.py
@@ -102,9 +102,18 @@
     return jnp.where(row < SHORT - 1, 0.0, keys * values)
 
 
+def split(array):
+    head = array.astype(jnp.bfloat16)
+    return head, (array - head.astype(jnp.float32)).astype(jnp.bfloat16)
+
+
+def weigh(left, right):
+    return jnp.dot(left, right, preferred_element_type=jnp.float32)
+
+
 def state_kernel(
     feat_hbm, taps_hbm, rates_hbm, residues_hbm, skip_hbm, send_ref, edge_ref, tables_ref,
-    feat_ref, taps_ref, rates_ref, residues_ref, skip_ref, product_ref, ends_ref, sems,
+    feat_ref, taps_ref, rates_ref, residues_ref, skip_ref, sems,
 ):
     copies = [
         pltpu.make_async_copy(source, target, sems.at[k])
@@ -139,6 +148,10 @@
         )
     ):
         tables_ref[pl.ds(k * modes, modes), :] = values
+    filters = rates.shape[1]
+    column = jnp.concatenate([rates[:, f : f + 1] for f in range(filters)], 0)
+    age = rows - 1 - lax.broadcasted_iota(jnp.int32, (filters * modes, rows), 1)
+    weights, weights_rest = split(jnp.exp(-column * age.astype(jnp.float32)))
     copies[2].wait()
     copies[3].wait()
     taps = [taps_ref[shift, j : j + 1, :] for j in range(3) for shift in range(SHORT)]
@@ -147,12 +160,12 @@
         taps + [skip_ref[...]] + unused, 0
     )
     copies[4].wait()
-    save(product_ref, inner_product(feat_ref, tables_ref, modes))
-    chunk_ends(product_ref, ends_ref, decay, rows)
+    product, product_rest = split(inner_product(feat_ref, tables_ref, modes))
+    every = weigh(weights, product) + (weigh(weights, product_rest) + weigh(weights_rest, product))
+    owner = lax.broadcasted_iota(jnp.int32, (modes, width), 1) // (width // filters)
     total = jnp.zeros((modes, width), jnp.float32)
-    for j in range(CHUNKS):
-        end = strided(ends_ref, modes * CHUNKS, width, j, modes, CHUNKS)
-        total = total * over_chunk + end
+    for f in range(filters):
+        total = jnp.where(owner == f, every[f * modes : (f + 1) * modes], total)
     edges = [
         feat_ref[j, pl.ds(first, EDGE), :].astype(jnp.float32)[at : at + 2]
         for first, at in ((0, 0), (rows - EDGE, EDGE - 2))
@@ -326,8 +339,6 @@
             pltpu.VMEM(rates.shape, f32),
             pltpu.VMEM(residues.shape, f32),
             pltpu.VMEM(skip.shape, f32),
-            by_row,
-            by_mode,
             pltpu.SemaphoreType.DMA((5,)),
         ],
         name="block_state",

time: 72.5 us -> 72.4 us (level)
  no operation moved by 1% of the time
where the time goes in v7:
time: 72.4 us; the launch traced here: 72.1 us
  blocking collectives  48.4 us (67%)
  starting transfers between devices  11.5 us (16%)
  Pallas kernels  4.92 us (7%)
  waiting for transfers between devices  4.65 us (6%)
  matrix products  1.58 us (2%)
  local copies, waits for them, and re-layouts  1 us (1%)
    all_gather x1, blocking collectives, shards(): lax.all_gather(coded.astype(jnp.float16), 'tp', axis=1, tiled=True)  48.4 us
    all_to_all x1, starting transfers between devices, shards(): lax.all_to_all(sent, 'ctx', split_axis=0, concat_axis=0, tiled=True)  9.45 us
    all_to_all x1, waiting for transfers between devices, shards(): lax.all_to_all(sent, 'ctx', split_axis=0, concat_axis=0, tiled=True)  3.67 us
    pallas_call x1, Pallas kernels, shards(): pl.pallas_call(state_kernel, in_specs=[pl.BlockSpec(memory_space=pltpu.HB...  2.48 us
    ppermute x1, starting transfers between devices, shards(): before = lax.ppermute(edge, 'ctx', [(i, i + 1) for i in range(blocks - 1)])  2.06 us
    dot_general x1, matrix products, shards(): mixed = jnp.dot(gated, out_weight, preferred_element_type=f32)  1.58 us
    pallas_call x1, Pallas kernels, shards(): pl.pallas_call(local_kernel, in_specs=[whole_in] * 2, out_specs=whole_in,...  1.48 us
  transfers between devices with their start and end apart: 2, of which 2 were waited for; matrix products, arithmetic and copies ran while one was open for 0% of the time, Pallas kernels for 2%

profile of v7, /device:TPU:2, one launch (start us, length us, event | category | flops | bytes accessed | tf_op | source)
XLA Modules:
  0.0 72.1 jit_solution(6030661565131874633)
XLA Ops:
  0.0 0.0 copy-start
  0.0 2.5 %block_state.1 = (bf16[32,48,128]{2,1,0:T(8,128)(2,1)}, bf16[16,256]{1,0:T(8,128)(2,1)}, f32[128,256]{1,0:T(8,128)S(1)}) custom-call(bf16[3,256,256]{2,1,0:T(8,128)(2,1)} %bitcast.3, f32[3,3,256]{2,1,0:T(4,128)} %taps_hbm.1, f32[16,16]{1,0:T(8,128)} %rates_hbm.1, f32[16,16]{1,0:T(8,128)} %residues_hbm.1, f32[1,256]{1,0:T(1,128)} %bitcast.5), custom_call_target="tpu_custom_call" | custom-call | tf_op jit(solution)/shard_map/block_state/pallas_call | solution.py:327
  2.5 9.5 %all-to-all-start = ((bf16[32,48,128]{2,1,0:T(8,128)(2,1)}), bf16[32,48,128]{2,1,0:T(8,128)(2,1)S(1)}, u32[]{:S(2)}, u32[]{:S(2)}) async-start(bf16[32,48,128]{2,1,0:T(8,128)(2,1)} %get-tuple-element.8), calls=%async_computation | async-start | bytes 786432 | tf_op jit(solution)/shard_map/all_to_all | solution.py:346
  11.9 2.1 %collective-permute-start = (bf16[16,256]{1,0:T(8,128)(2,1)}, bf16[16,256]{1,0:T(8,128)(2,1)S(1)}, u32[]{:S(2)}, u32[]{:S(2)}) collective-permute-start(bf16[16,256]{1,0:T(8,128)(2,1)} %get-tuple-element.9), channel_id=1, source_target_pairs={{0,16},{16,32},{32,48},{48,64},{64,80},{80,96},{96,112},{112,128},... | collective-permute-start | bytes 24584 | tf_op jit(solution)/shard_map/ppermute | solution.py:347
  14.0 0.0 copy-start.1
  14.0 1.0 %copy-done.1 = bf16[256,3,256]{2,0,1:T(8,128)(2,1)S(1)} copy-done((bf16[256,3,256]{2,0,1:T(8,128)(2,1)S(1)}, bf16[256,3,256]{2,0,1:T(8,128)(2,1)}, u32[]{:S(2)}) %copy-start.1) | copy-done | bytes 393240
  15.0 1.5 %local_conv.1.local_ref = f32[640,256]{1,0:T(8,128)S(1)} custom-call(bf16[3,256,256]{2,1,0:T(8,128)(2,1)S(1)} %bitcast.4, f32[128,256]{1,0:T(8,128)S(1)} %get-tuple-element.10.tables_ref), custom_call_target="tpu_custom_call" | custom-call | tf_op jit(solution)/shard_map/local_conv/pallas_call | solution.py:348
  16.5 1.0 %collective-permute-done.edge_ref = bf16[16,256]{1,0:T(8,128)(2,1)S(1)} collective-permute-done((bf16[16,256]{1,0:T(8,128)(2,1)}, bf16[16,256]{1,0:T(8,128)(2,1)S(1)}, u32[]{:S(2)}, u32[]{:S(2)}) %collective-permute-start) | collective-permute-done | bytes 8224 | tf_op jit(solution)/shard_map/ppermute | solution.py:347
  17.5 3.7 %all-to-all-done.recv_ref = bf16[32,48,128]{2,1,0:T(8,128)(2,1)S(1)} async-done(((bf16[32,48,128]{2,1,0:T(8,128)(2,1)}), bf16[32,48,128]{2,1,0:T(8,128)(2,1)S(1)}, u32[]{:S(2)}, u32[]{:S(2)}) %all-to-all-start) | async-done | bytes 393248 | tf_op jit(solution)/shard_map/all_to_all | solution.py:346
  21.1 1.0 %carry_gate.1 = f32[256,256]{1,0:T(8,128)S(1)} custom-call(bf16[32,48,128]{2,1,0:T(8,128)(2,1)S(1)} %all-to-all-done.recv_ref, bf16[16,256]{1,0:T(8,128)(2,1)S(1)} %collective-permute-done.edge_ref, f32[640,256]{1,0:T(8,128)S(1)} %local_conv.1.local_ref), custom_call_target="tpu_custom_call" | custom-call | tf_op jit(solution)/shard_map/carry_gate/pallas_call | solution.py:357
  22.1 48.4 %all-gather.1 = f16[256,4096]{1,0:T(8,128)(2,1)S(1)} all-gather(f16[256,256]{1,0:T(8,128)(2,1)S(1)} %convert_element_type.12), channel_id=1, replica_groups=mesh['ctx'=32,'tp'=16] {'tp'}, dimensions={1}, use_global_device_ids=true | all-gather | bytes 2228224 | tf_op jit(solution)/shard_map/all_gather | solution.py:371
  70.6 0.0 copy-done
  70.6 1.6 %fusion.7 = bf16[256,256]{1,0:T(8,128)(2,1)} fusion(bf16[4096,256]{1,0:T(8,128)(2,1)S(1)} %copy-done, f16[256,4096]{1,0:T(8,128)(2,1)S(1)} %all-gather.1), kind=kOutput, calls=%fused_computation.6 | convolution fusion | flops 543293440 | bytes 4325376 | tf_op jit(solution)/shard_map/dot_general | solution.py:374
  (1 shorter events, 0.0 us)
Async XLA Ops:
  0.0 70.6 %copy-start = (bf16[4096,256]{1,0:T(8,128)(2,1)S(1)}, bf16[4096,256]{1,0:T(8,128)(2,1)}, u32[]{:S(2)}) copy-start(bf16[4096,256]{1,0:T(8,128)(2,1)} %param.11) | copy-start | bytes 6291460
  2.5 18.7 %all-to-all-start = ((bf16[32,48,128]{2,1,0:T(8,128)(2,1)}), bf16[32,48,128]{2,1,0:T(8,128)(2,1)S(1)}, u32[]{:S(2)}, u32[]{:S(2)}) async-start(bf16[32,48,128]{2,1,0:T(8,128)(2,1)} %get-tuple-element.8), calls=%async_computation | async-start | bytes 786432 | tf_op jit(solution)/shard_map/all_to_all | solution.py:346
  11.9 5.5 %collective-permute-start = (bf16[16,256]{1,0:T(8,128)(2,1)}, bf16[16,256]{1,0:T(8,128)(2,1)S(1)}, u32[]{:S(2)}, u32[]{:S(2)}) collective-permute-start(bf16[16,256]{1,0:T(8,128)(2,1)} %get-tuple-element.9), channel_id=1, source_target_pairs={{0,16},{16,32},{32,48},{48,64},{64,80},{80,96},{96,112},{112,128},... | collective-permute-start | bytes 24584 | tf_op jit(solution)/shard_map/ppermute | solution.py:347
  14.0 1.0 %copy-start.1 = (bf16[256,3,256]{2,0,1:T(8,128)(2,1)S(1)}, bf16[256,3,256]{2,0,1:T(8,128)(2,1)}, u32[]{:S(2)}) copy-start(bf16[256,3,256]{2,0,1:T(8,128)(2,1)} %param.6) | copy-start | bytes 1179652

commit v8 on v7

--- a/solution.py
+++ b/solution.py
@@ -112,7 +112,7 @@
 
 
 def state_kernel(
-    feat_hbm, taps_hbm, rates_hbm, residues_hbm, skip_hbm, send_ref, edge_ref, tables_ref,
+    feat_hbm, taps_hbm, rates_hbm, residues_hbm, skip_hbm, send_ref, tables_ref,
     feat_ref, taps_ref, rates_ref, residues_ref, skip_ref, sems,
 ):
     copies = [
@@ -176,12 +176,13 @@
         [a[:, t * LANES : (t + 1) * LANES] for a in (total, edges) for t in range(width // LANES)], 0
     )
     block = block.astype(jnp.bfloat16)
-    edge_ref[...] = feat_ref[0, pl.ds(rows - EDGE, EDGE), :]
     for e in range(send_ref.shape[0]):
         send_ref[e] = block
 
 
-def local_kernel(feat_ref, tables_ref, local_ref, product_ref, states_ref, conv_ref):
+def local_kernel(
+    feat_ref, tables_ref, local_ref, edge_ref, product_ref, states_ref, conv_ref
+):
     rows, width = feat_ref.shape[1:]
     modes = tables_ref.shape[0] // (TABLES + 1)
     steps = rows // CHUNKS
@@ -214,6 +215,7 @@
         recur(product_ref, t * rows, part, begin, steps, visit)
     skip = single(tables_ref, modes, 3 * SHORT)
     local_ref[pl.ds(2 * rows, (TABLES + 1) * modes), :] = tables_ref[...]
+    edge_ref[...] = feat_ref[0, pl.ds(rows - EDGE, EDGE), :]
     local_ref[pl.ds(0, rows), :] = query
     local_ref[pl.ds(rows, rows), :] = query * (whole(conv_ref, rows, width) + skip * product)
 
@@ -324,13 +326,12 @@
     by_row = pltpu.VMEM((tiles * rows, LANES), f32)
     by_mode = pltpu.VMEM((tiles * modes * CHUNKS, LANES), f32)
     whole_in = pl.BlockSpec(memory_space=pltpu.VMEM)
-    sent, edge, tables = pl.pallas_call(
+    sent, tables = pl.pallas_call(
         state_kernel,
         in_specs=[pl.BlockSpec(memory_space=pltpu.HBM)] * 5,
-        out_specs=(whole_in,) * 3,
+        out_specs=(whole_in,) * 2,
         out_shape=(
             jax.ShapeDtypeStruct((blocks, payload, LANES), jnp.bfloat16),
-            jax.ShapeDtypeStruct((EDGE, width), jnp.bfloat16),
             pltpu.VMEM(((TABLES + 1) * modes, width), f32),
         ),
         scratch_shapes=[
@@ -344,16 +345,19 @@
         name="block_state",
     )(feats, short_taps, rates, residues, skip)
     received = lax.all_to_all(sent, "ctx", split_axis=0, concat_axis=0, tiled=True)
-    before = lax.ppermute(edge, "ctx", [(i, i + 1) for i in range(blocks - 1)])
-    local = pl.pallas_call(
+    local, edge = pl.pallas_call(
         local_kernel,
         in_specs=[whole_in] * 2,
-        out_specs=whole_in,
-        out_shape=jax.ShapeDtypeStruct((2 * rows + (TABLES + 1) * modes, width), f32),
+        out_specs=(whole_in,) * 2,
+        out_shape=(
+            jax.ShapeDtypeStruct((2 * rows + (TABLES + 1) * modes, width), f32),
+            jax.ShapeDtypeStruct((EDGE, width), jnp.bfloat16),
+        ),
         scratch_shapes=[by_row, by_mode, by_row],
         compiler_params=pltpu.CompilerParams(vmem_limit_bytes=KERNEL_VMEM),
         name="local_conv",
     )(feats, tables)
+    before = lax.ppermute(edge, "ctx", [(i, i + 1) for i in range(blocks - 1)])
     coded = pl.pallas_call(
         carry_kernel,
         in_specs=[whole_in] * 3,

time: 72.4 us -> 72.4 us (level)
    all_to_all x1, waiting for transfers between devices: 3.67 us -> 1.74 us  [shards(): lax.all_to_all(sent, 'ctx', split_axis=0, concat_axis=0, tiled=True)]
    ppermute x1, waiting for transfers between devices: 0.97 us -> 2.9 us  [shards(): before = lax.ppermute(edge, 'ctx', [(i, i + 1) for i in range(blocks - 1)])]
where the time goes in v8:
time: 72.4 us; the launch traced here: 72.2 us
  blocking collectives  48.4 us (67%)
  starting transfers between devices  11.5 us (16%)
  Pallas kernels  4.93 us (7%)
  waiting for transfers between devices  4.64 us (6%)
  matrix products  1.58 us (2%)
  local copies, waits for them, and re-layouts  1 us (1%)
    all_gather x1, blocking collectives, shards(): lax.all_gather(coded.astype(jnp.float16), 'tp', axis=1, tiled=True)  48.4 us
    all_to_all x1, starting transfers between devices, shards(): lax.all_to_all(sent, 'ctx', split_axis=0, concat_axis=0, tiled=True)  9.46 us
    ppermute x1, waiting for transfers between devices, shards(): before = lax.ppermute(edge, 'ctx', [(i, i + 1) for i in range(blocks - 1)])  2.9 us
    pallas_call x1, Pallas kernels, shards(): pl.pallas_call(state_kernel, in_specs=[pl.BlockSpec(memory_space=pltpu.HB...  2.48 us
    ppermute x1, starting transfers between devices, shards(): before = lax.ppermute(edge, 'ctx', [(i, i + 1) for i in range(blocks - 1)])  2.06 us
    all_to_all x1, waiting for transfers between devices, shards(): lax.all_to_all(sent, 'ctx', split_axis=0, concat_axis=0, tiled=True)  1.74 us
    dot_general x1, matrix products, shards(): mixed = jnp.dot(gated, out_weight, preferred_element_type=f32)  1.58 us
    pallas_call x1, Pallas kernels, shards(): pl.pallas_call(local_kernel, in_specs=[whole_in] * 2, out_specs=(whole_in...  1.48 us
  transfers between devices with their start and end apart: 2, of which 2 were waited for; matrix products, arithmetic and copies ran while one was open for 0% of the time, Pallas kernels for 2%

profile of v8, /device:TPU:2, one launch (start us, length us, event | category | flops | bytes accessed | tf_op | source)
XLA Modules:
  0.0 72.2 jit_solution(5690866850556655120)
XLA Ops:
  0.0 0.0 copy-start
  0.0 2.5 %block_state.1 = (bf16[32,48,128]{2,1,0:T(8,128)(2,1)}, f32[128,256]{1,0:T(8,128)S(1)}) custom-call(bf16[3,256,256]{2,1,0:T(8,128)(2,1)} %bitcast.3, f32[3,3,256]{2,1,0:T(4,128)} %taps_hbm.1, f32[16,16]{1,0:T(8,128)} %rates_hbm.1, f32[16,16]{1,0:T(8,128)} %residues_hbm.1, f32[1,256]{1,0:T(1,128)} %bitcast.5), custom_call_target="tpu_custom_call" | custom-call | tf_op jit(solution)/shard_map/block_state/pallas_call | solution.py:329
  2.5 9.5 %all-to-all-start = ((bf16[32,48,128]{2,1,0:T(8,128)(2,1)}), bf16[32,48,128]{2,1,0:T(8,128)(2,1)S(1)}, u32[]{:S(2)}, u32[]{:S(2)}) async-start(bf16[32,48,128]{2,1,0:T(8,128)(2,1)} %get-tuple-element.9), calls=%async_computation | async-start | bytes 786432 | tf_op jit(solution)/shard_map/all_to_all | solution.py:347
  12.0 0.0 copy-start.1
  12.0 1.0 %copy-done.1 = bf16[256,3,256]{2,0,1:T(8,128)(2,1)S(1)} copy-done((bf16[256,3,256]{2,0,1:T(8,128)(2,1)S(1)}, bf16[256,3,256]{2,0,1:T(8,128)(2,1)}, u32[]{:S(2)}) %copy-start.1) | copy-done | bytes 393240
  13.0 1.5 %local_conv.1 = (f32[640,256]{1,0:T(8,128)S(1)}, bf16[16,256]{1,0:T(8,128)(2,1)S(1)}) custom-call(bf16[3,256,256]{2,1,0:T(8,128)(2,1)S(1)} %bitcast.4, f32[128,256]{1,0:T(8,128)S(1)} %get-tuple-element.10.tables_ref), custom_call_target="tpu_custom_call" | custom-call | tf_op jit(solution)/shard_map/local_conv/pallas_call | solution.py:348
  14.4 2.1 %collective-permute-start = (bf16[16,256]{1,0:T(8,128)(2,1)S(1)}, bf16[16,256]{1,0:T(8,128)(2,1)S(1)}, u32[]{:S(2)}, u32[]{:S(2)}) collective-permute-start(bf16[16,256]{1,0:T(8,128)(2,1)S(1)} %get-tuple-element.11), channel_id=1, source_target_pairs={{0,16},{16,32},{32,48},{48,64},{64,80},{80,96},{96,112},{112,128},... | collective-permute-start | bytes 24584 | tf_op jit(solution)/shard_map/ppermute | solution.py:360
  16.5 2.9 %collective-permute-done.edge_ref = bf16[16,256]{1,0:T(8,128)(2,1)S(1)} collective-permute-done((bf16[16,256]{1,0:T(8,128)(2,1)S(1)}, bf16[16,256]{1,0:T(8,128)(2,1)S(1)}, u32[]{:S(2)}, u32[]{:S(2)}) %collective-permute-start) | collective-permute-done | bytes 8224 | tf_op jit(solution)/shard_map/ppermute | solution.py:360
  19.4 1.7 %all-to-all-done.recv_ref = bf16[32,48,128]{2,1,0:T(8,128)(2,1)S(1)} async-done(((bf16[32,48,128]{2,1,0:T(8,128)(2,1)}), bf16[32,48,128]{2,1,0:T(8,128)(2,1)S(1)}, u32[]{:S(2)}, u32[]{:S(2)}) %all-to-all-start) | async-done | bytes 393248 | tf_op jit(solution)/shard_map/all_to_all | solution.py:347
  21.2 1.0 %carry_gate.1 = f32[256,256]{1,0:T(8,128)S(1)} custom-call(bf16[32,48,128]{2,1,0:T(8,128)(2,1)S(1)} %all-to-all-done.recv_ref, bf16[16,256]{1,0:T(8,128)(2,1)S(1)} %collective-permute-done.edge_ref, f32[640,256]{1,0:T(8,128)S(1)} %get-tuple-element.12.local_ref), custom_call_target="tpu_custom_call" | custom-call | tf_op jit(solution)/shard_map/carry_gate/pallas_call | solution.py:361
  22.2 48.4 %all-gather.1 = f16[256,4096]{1,0:T(8,128)(2,1)S(1)} all-gather(f16[256,256]{1,0:T(8,128)(2,1)S(1)} %convert_element_type.12), channel_id=1, replica_groups=mesh['ctx'=32,'tp'=16] {'tp'}, dimensions={1}, use_global_device_ids=true | all-gather | bytes 2228224 | tf_op jit(solution)/shard_map/all_gather | solution.py:375
  70.6 0.0 copy-done
  70.6 1.6 %fusion.7 = bf16[256,256]{1,0:T(8,128)(2,1)} fusion(bf16[4096,256]{1,0:T(8,128)(2,1)S(1)} %copy-done, f16[256,4096]{1,0:T(8,128)(2,1)S(1)} %all-gather.1), kind=kOutput, calls=%fused_computation.6 | convolution fusion | flops 543293440 | bytes 4325376 | tf_op jit(solution)/shard_map/dot_general | solution.py:378
  (1 shorter events, 0.0 us)
Async XLA Ops:
  0.0 70.6 %copy-start = (bf16[4096,256]{1,0:T(8,128)(2,1)S(1)}, bf16[4096,256]{1,0:T(8,128)(2,1)}, u32[]{:S(2)}) copy-start(bf16[4096,256]{1,0:T(8,128)(2,1)} %param.11) | copy-start | bytes 6291460
  2.5 18.7 %all-to-all-start = ((bf16[32,48,128]{2,1,0:T(8,128)(2,1)}), bf16[32,48,128]{2,1,0:T(8,128)(2,1)S(1)}, u32[]{:S(2)}, u32[]{:S(2)}) async-start(bf16[32,48,128]{2,1,0:T(8,128)(2,1)} %get-tuple-element.9), calls=%async_computation | async-start | bytes 786432 | tf_op jit(solution)/shard_map/all_to_all | solution.py:347
  12.0 1.0 %copy-start.1 = (bf16[256,3,256]{2,0,1:T(8,128)(2,1)S(1)}, bf16[256,3,256]{2,0,1:T(8,128)(2,1)}, u32[]{:S(2)}) copy-start(bf16[256,3,256]{2,0,1:T(8,128)(2,1)} %param.6) | copy-start | bytes 1179652
  14.4 5.0 %collective-permute-start = (bf16[16,256]{1,0:T(8,128)(2,1)S(1)}, bf16[16,256]{1,0:T(8,128)(2,1)S(1)}, u32[]{:S(2)}, u32[]{:S(2)}) collective-permute-start(bf16[16,256]{1,0:T(8,128)(2,1)S(1)} %get-tuple-element.11), channel_id=1, source_target_pairs={{0,16},{16,32},{32,48},{48,64},{64,80},{80,96},{96,112},{112,128},... | collective-permute-start | bytes 24584 | tf_op jit(solution)/shard_map/ppermute | solution.py:360

commit v9 on v8

--- a/solution.py
+++ b/solution.py
@@ -303,7 +303,7 @@
             conv_ref[where, :] = functools.reduce(jnp.add, carry)
             return carry
 
-        lax.fori_loop(0, steps, step, begin, unroll=4)
+        lax.fori_loop(0, steps, step, begin, unroll=16)
     query, base = local_ref[pl.ds(0, rows), :], local_ref[pl.ds(rows, rows), :]
     gated = base + query * whole(conv_ref, rows, width)
     row = lax.broadcasted_iota(jnp.int32, (rows, width), 0)

time: 72.4 us -> 72.3 us (level)
  no operation moved by 1% of the time
where the time goes in v9:
time: 72.3 us; the launch traced here: 72 us
  blocking collectives  48.4 us (67%)
  starting transfers between devices  11.5 us (16%)
  Pallas kernels  4.8 us (7%)
  waiting for transfers between devices  4.64 us (6%)
  matrix products  1.58 us (2%)
  local copies, waits for them, and re-layouts  1 us (1%)
    all_gather x1, blocking collectives, shards(): lax.all_gather(coded.astype(jnp.float16), 'tp', axis=1, tiled=True)  48.4 us
    all_to_all x1, starting transfers between devices, shards(): lax.all_to_all(sent, 'ctx', split_axis=0, concat_axis=0, tiled=True)  9.46 us
    ppermute x1, waiting for transfers between devices, shards(): before = lax.ppermute(edge, 'ctx', [(i, i + 1) for i in range(blocks - 1)])  2.9 us
    pallas_call x1, Pallas kernels, shards(): pl.pallas_call(state_kernel, in_specs=[pl.BlockSpec(memory_space=pltpu.HB...  2.48 us
    ppermute x1, starting transfers between devices, shards(): before = lax.ppermute(edge, 'ctx', [(i, i + 1) for i in range(blocks - 1)])  2.06 us
    all_to_all x1, waiting for transfers between devices, shards(): lax.all_to_all(sent, 'ctx', split_axis=0, concat_axis=0, tiled=True)  1.74 us
    dot_general x1, matrix products, shards(): mixed = jnp.dot(gated, out_weight, preferred_element_type=f32)  1.58 us
    pallas_call x1, Pallas kernels, shards(): pl.pallas_call(local_kernel, in_specs=[whole_in] * 2, out_specs=(whole_in...  1.48 us
  transfers between devices with their start and end apart: 2, of which 2 were waited for; matrix products, arithmetic and copies ran while one was open for 0% of the time, Pallas kernels for 2%

profile of v9, /device:TPU:2, one launch (start us, length us, event | category | flops | bytes accessed | tf_op | source)
XLA Modules:
  0.0 72.0 jit_solution(13385417431894848081)
XLA Ops:
  0.0 0.0 copy-start
  0.0 2.5 %block_state.1 = (bf16[32,48,128]{2,1,0:T(8,128)(2,1)}, f32[128,256]{1,0:T(8,128)S(1)}) custom-call(bf16[3,256,256]{2,1,0:T(8,128)(2,1)} %bitcast.3, f32[3,3,256]{2,1,0:T(4,128)} %taps_hbm.1, f32[16,16]{1,0:T(8,128)} %rates_hbm.1, f32[16,16]{1,0:T(8,128)} %residues_hbm.1, f32[1,256]{1,0:T(1,128)} %bitcast.5), custom_call_target="tpu_custom_call" | custom-call | tf_op jit(solution)/shard_map/block_state/pallas_call | solution.py:329
  2.5 9.5 %all-to-all-start = ((bf16[32,48,128]{2,1,0:T(8,128)(2,1)}), bf16[32,48,128]{2,1,0:T(8,128)(2,1)S(1)}, u32[]{:S(2)}, u32[]{:S(2)}) async-start(bf16[32,48,128]{2,1,0:T(8,128)(2,1)} %get-tuple-element.9), calls=%async_computation | async-start | bytes 786432 | tf_op jit(solution)/shard_map/all_to_all | solution.py:347
  12.0 0.0 copy-start.1
  12.0 1.0 %copy-done.1 = bf16[256,3,256]{2,0,1:T(8,128)(2,1)S(1)} copy-done((bf16[256,3,256]{2,0,1:T(8,128)(2,1)S(1)}, bf16[256,3,256]{2,0,1:T(8,128)(2,1)}, u32[]{:S(2)}) %copy-start.1) | copy-done | bytes 393240
  13.0 1.5 %local_conv.1 = (f32[640,256]{1,0:T(8,128)S(1)}, bf16[16,256]{1,0:T(8,128)(2,1)S(1)}) custom-call(bf16[3,256,256]{2,1,0:T(8,128)(2,1)S(1)} %bitcast.4, f32[128,256]{1,0:T(8,128)S(1)} %get-tuple-element.10.tables_ref), custom_call_target="tpu_custom_call" | custom-call | tf_op jit(solution)/shard_map/local_conv/pallas_call | solution.py:348
  14.4 2.1 %collective-permute-start = (bf16[16,256]{1,0:T(8,128)(2,1)S(1)}, bf16[16,256]{1,0:T(8,128)(2,1)S(1)}, u32[]{:S(2)}, u32[]{:S(2)}) collective-permute-start(bf16[16,256]{1,0:T(8,128)(2,1)S(1)} %get-tuple-element.11), channel_id=1, source_target_pairs={{0,16},{16,32},{32,48},{48,64},{64,80},{80,96},{96,112},{112,128},... | collective-permute-start | bytes 24584 | tf_op jit(solution)/shard_map/ppermute | solution.py:360
  16.5 2.9 %collective-permute-done.edge_ref = bf16[16,256]{1,0:T(8,128)(2,1)S(1)} collective-permute-done((bf16[16,256]{1,0:T(8,128)(2,1)S(1)}, bf16[16,256]{1,0:T(8,128)(2,1)S(1)}, u32[]{:S(2)}, u32[]{:S(2)}) %collective-permute-start) | collective-permute-done | bytes 8224 | tf_op jit(solution)/shard_map/ppermute | solution.py:360
  19.4 1.7 %all-to-all-done.recv_ref = bf16[32,48,128]{2,1,0:T(8,128)(2,1)S(1)} async-done(((bf16[32,48,128]{2,1,0:T(8,128)(2,1)}), bf16[32,48,128]{2,1,0:T(8,128)(2,1)S(1)}, u32[]{:S(2)}, u32[]{:S(2)}) %all-to-all-start) | async-done | bytes 393248 | tf_op jit(solution)/shard_map/all_to_all | solution.py:347
  21.2 0.8 %carry_gate.1 = f32[256,256]{1,0:T(8,128)S(1)} custom-call(bf16[32,48,128]{2,1,0:T(8,128)(2,1)S(1)} %all-to-all-done.recv_ref, bf16[16,256]{1,0:T(8,128)(2,1)S(1)} %collective-permute-done.edge_ref, f32[640,256]{1,0:T(8,128)S(1)} %get-tuple-element.12.local_ref), custom_call_target="tpu_custom_call" | custom-call | tf_op jit(solution)/shard_map/carry_gate/pallas_call | solution.py:361
  22.0 48.4 %all-gather.1 = f16[256,4096]{1,0:T(8,128)(2,1)S(1)} all-gather(f16[256,256]{1,0:T(8,128)(2,1)S(1)} %convert_element_type.12), channel_id=1, replica_groups=mesh['ctx'=32,'tp'=16] {'tp'}, dimensions={1}, use_global_device_ids=true | all-gather | bytes 2228224 | tf_op jit(solution)/shard_map/all_gather | solution.py:375
  70.4 0.0 copy-done
  70.4 1.6 %fusion.7 = bf16[256,256]{1,0:T(8,128)(2,1)} fusion(bf16[4096,256]{1,0:T(8,128)(2,1)S(1)} %copy-done, f16[256,4096]{1,0:T(8,128)(2,1)S(1)} %all-gather.1), kind=kOutput, calls=%fused_computation.6 | convolution fusion | flops 543293440 | bytes 4325376 | tf_op jit(solution)/shard_map/dot_general | solution.py:378
  (1 shorter events, 0.0 us)
Async XLA Ops:
  0.0 70.4 %copy-start = (bf16[4096,256]{1,0:T(8,128)(2,1)S(1)}, bf16[4096,256]{1,0:T(8,128)(2,1)}, u32[]{:S(2)}) copy-start(bf16[4096,256]{1,0:T(8,128)(2,1)} %param.11) | copy-start | bytes 6291460
  2.5 18.7 %all-to-all-start = ((bf16[32,48,128]{2,1,0:T(8,128)(2,1)}), bf16[32,48,128]{2,1,0:T(8,128)(2,1)S(1)}, u32[]{:S(2)}, u32[]{:S(2)}) async-start(bf16[32,48,128]{2,1,0:T(8,128)(2,1)} %get-tuple-element.9), calls=%async_computation | async-start | bytes 786432 | tf_op jit(solution)/shard_map/all_to_all | solution.py:347
  12.0 1.0 %copy-start.1 = (bf16[256,3,256]{2,0,1:T(8,128)(2,1)S(1)}, bf16[256,3,256]{2,0,1:T(8,128)(2,1)}, u32[]{:S(2)}) copy-start(bf16[256,3,256]{2,0,1:T(8,128)(2,1)} %param.6) | copy-start | bytes 1179652
  14.4 5.0 %collective-permute-start = (bf16[16,256]{1,0:T(8,128)(2,1)S(1)}, bf16[16,256]{1,0:T(8,128)(2,1)S(1)}, u32[]{:S(2)}, u32[]{:S(2)}) collective-permute-start(bf16[16,256]{1,0:T(8,128)(2,1)S(1)} %get-tuple-element.11), channel_id=1, source_target_pairs={{0,16},{16,32},{32,48},{48,64},{64,80},{80,96},{96,112},{112,128},... | collective-permute-start | bytes 24584 | tf_op jit(solution)/shard_map/ppermute | solution.py:360

commit v10 on v8

--- a/solution.py
+++ b/solution.py
@@ -120,7 +120,7 @@
         for k, (source, target) in enumerate(
             (
                 (rates_hbm, rates_ref), (residues_hbm, residues_ref), (taps_hbm, taps_ref),
-                (skip_hbm, skip_ref), (feat_hbm, feat_ref),
+                (skip_hbm, skip_ref), (feat_hbm.at[pl.ds(1, 2)], feat_ref.at[pl.ds(1, 2)]),
             )
         )
     ]

time: 72.4 us -> 72.4 us (level)
  no operation moved by 1% of the time
where the time goes in v10:
time: 72.4 us; the launch traced here: 72.1 us
  blocking collectives  48.4 us (67%)
  starting transfers between devices  11.5 us (16%)
  Pallas kernels  4.89 us (7%)
  waiting for transfers between devices  4.64 us (6%)
  matrix products  1.59 us (2%)
  local copies, waits for them, and re-layouts  1 us (1%)
    all_gather x1, blocking collectives, shards(): lax.all_gather(coded.astype(jnp.float16), 'tp', axis=1, tiled=True)  48.4 us
    all_to_all x1, starting transfers between devices, shards(): lax.all_to_all(sent, 'ctx', split_axis=0, concat_axis=0, tiled=True)  9.46 us
    ppermute x1, waiting for transfers between devices, shards(): before = lax.ppermute(edge, 'ctx', [(i, i + 1) for i in range(blocks - 1)])  2.9 us
    pallas_call x1, Pallas kernels, shards(): pl.pallas_call(state_kernel, in_specs=[pl.BlockSpec(memory_space=pltpu.HB...  2.44 us
    ppermute x1, starting transfers between devices, shards(): before = lax.ppermute(edge, 'ctx', [(i, i + 1) for i in range(blocks - 1)])  2.06 us
    all_to_all x1, waiting for transfers between devices, shards(): lax.all_to_all(sent, 'ctx', split_axis=0, concat_axis=0, tiled=True)  1.74 us
    dot_general x1, matrix products, shards(): mixed = jnp.dot(gated, out_weight, preferred_element_type=f32)  1.59 us
    pallas_call x1, Pallas kernels, shards(): pl.pallas_call(local_kernel, in_specs=[whole_in] * 2, out_specs=(whole_in...  1.48 us
  transfers between devices with their start and end apart: 2, of which 2 were waited for; matrix products, arithmetic and copies ran while one was open for 0% of the time, Pallas kernels for 2%

profile of v10, /device:TPU:2, one launch (start us, length us, event | category | flops | bytes accessed | tf_op | source)
XLA Modules:
  0.0 72.1 jit_solution(5405862233261438796)
XLA Ops:
  0.0 0.0 copy-start
  0.0 2.4 %block_state.1 = (bf16[32,48,128]{2,1,0:T(8,128)(2,1)}, f32[128,256]{1,0:T(8,128)S(1)}) custom-call(bf16[3,256,256]{2,1,0:T(8,128)(2,1)} %bitcast.3, f32[3,3,256]{2,1,0:T(4,128)} %taps_hbm.1, f32[16,16]{1,0:T(8,128)} %rates_hbm.1, f32[16,16]{1,0:T(8,128)} %residues_hbm.1, f32[1,256]{1,0:T(1,128)} %bitcast.5), custom_call_target="tpu_custom_call" | custom-call | tf_op jit(solution)/shard_map/block_state/pallas_call | solution.py:329
  2.4 9.5 %all-to-all-start = ((bf16[32,48,128]{2,1,0:T(8,128)(2,1)}), bf16[32,48,128]{2,1,0:T(8,128)(2,1)S(1)}, u32[]{:S(2)}, u32[]{:S(2)}) async-start(bf16[32,48,128]{2,1,0:T(8,128)(2,1)} %get-tuple-element.9), calls=%async_computation | async-start | bytes 786432 | tf_op jit(solution)/shard_map/all_to_all | solution.py:347
  11.9 0.0 copy-start.1
  11.9 1.0 %copy-done.1 = bf16[256,3,256]{2,0,1:T(8,128)(2,1)S(1)} copy-done((bf16[256,3,256]{2,0,1:T(8,128)(2,1)S(1)}, bf16[256,3,256]{2,0,1:T(8,128)(2,1)}, u32[]{:S(2)}) %copy-start.1) | copy-done | bytes 393240
  12.9 1.5 %local_conv.1 = (f32[640,256]{1,0:T(8,128)S(1)}, bf16[16,256]{1,0:T(8,128)(2,1)S(1)}) custom-call(bf16[3,256,256]{2,1,0:T(8,128)(2,1)S(1)} %bitcast.4, f32[128,256]{1,0:T(8,128)S(1)} %get-tuple-element.10.tables_ref), custom_call_target="tpu_custom_call" | custom-call | tf_op jit(solution)/shard_map/local_conv/pallas_call | solution.py:348
  14.4 2.1 %collective-permute-start = (bf16[16,256]{1,0:T(8,128)(2,1)S(1)}, bf16[16,256]{1,0:T(8,128)(2,1)S(1)}, u32[]{:S(2)}, u32[]{:S(2)}) collective-permute-start(bf16[16,256]{1,0:T(8,128)(2,1)S(1)} %get-tuple-element.11), channel_id=1, source_target_pairs={{0,16},{16,32},{32,48},{48,64},{64,80},{80,96},{96,112},{112,128},... | collective-permute-start | bytes 24584 | tf_op jit(solution)/shard_map/ppermute | solution.py:360
  16.5 2.9 %collective-permute-done.edge_ref = bf16[16,256]{1,0:T(8,128)(2,1)S(1)} collective-permute-done((bf16[16,256]{1,0:T(8,128)(2,1)S(1)}, bf16[16,256]{1,0:T(8,128)(2,1)S(1)}, u32[]{:S(2)}, u32[]{:S(2)}) %collective-permute-start) | collective-permute-done | bytes 8224 | tf_op jit(solution)/shard_map/ppermute | solution.py:360
  19.4 1.7 %all-to-all-done.recv_ref = bf16[32,48,128]{2,1,0:T(8,128)(2,1)S(1)} async-done(((bf16[32,48,128]{2,1,0:T(8,128)(2,1)}), bf16[32,48,128]{2,1,0:T(8,128)(2,1)S(1)}, u32[]{:S(2)}, u32[]{:S(2)}) %all-to-all-start) | async-done | bytes 393248 | tf_op jit(solution)/shard_map/all_to_all | solution.py:347
  21.1 1.0 %carry_gate.1 = f32[256,256]{1,0:T(8,128)S(1)} custom-call(bf16[32,48,128]{2,1,0:T(8,128)(2,1)S(1)} %all-to-all-done.recv_ref, bf16[16,256]{1,0:T(8,128)(2,1)S(1)} %collective-permute-done.edge_ref, f32[640,256]{1,0:T(8,128)S(1)} %get-tuple-element.12.local_ref), custom_call_target="tpu_custom_call" | custom-call | tf_op jit(solution)/shard_map/carry_gate/pallas_call | solution.py:361
  22.1 48.4 %all-gather.1 = f16[256,4096]{1,0:T(8,128)(2,1)S(1)} all-gather(f16[256,256]{1,0:T(8,128)(2,1)S(1)} %convert_element_type.12), channel_id=1, replica_groups=mesh['ctx'=32,'tp'=16] {'tp'}, dimensions={1}, use_global_device_ids=true | all-gather | bytes 2228224 | tf_op jit(solution)/shard_map/all_gather | solution.py:375
  70.5 0.0 copy-done
  70.5 1.6 %fusion.7 = bf16[256,256]{1,0:T(8,128)(2,1)} fusion(bf16[4096,256]{1,0:T(8,128)(2,1)S(1)} %copy-done, f16[256,4096]{1,0:T(8,128)(2,1)S(1)} %all-gather.1), kind=kOutput, calls=%fused_computation.6 | convolution fusion | flops 543293440 | bytes 4325376 | tf_op jit(solution)/shard_map/dot_general | solution.py:378
  (1 shorter events, 0.0 us)
Async XLA Ops:
  0.0 70.5 %copy-start = (bf16[4096,256]{1,0:T(8,128)(2,1)S(1)}, bf16[4096,256]{1,0:T(8,128)(2,1)}, u32[]{:S(2)}) copy-start(bf16[4096,256]{1,0:T(8,128)(2,1)} %param.11) | copy-start | bytes 6291460
  2.4 18.7 %all-to-all-start = ((bf16[32,48,128]{2,1,0:T(8,128)(2,1)}), bf16[32,48,128]{2,1,0:T(8,128)(2,1)S(1)}, u32[]{:S(2)}, u32[]{:S(2)}) async-start(bf16[32,48,128]{2,1,0:T(8,128)(2,1)} %get-tuple-element.9), calls=%async_computation | async-start | bytes 786432 | tf_op jit(solution)/shard_map/all_to_all | solution.py:347
  11.9 1.0 %copy-start.1 = (bf16[256,3,256]{2,0,1:T(8,128)(2,1)S(1)}, bf16[256,3,256]{2,0,1:T(8,128)(2,1)}, u32[]{:S(2)}) copy-start(bf16[256,3,256]{2,0,1:T(8,128)(2,1)} %param.6) | copy-start | bytes 1179652
  14.4 5.0 %collective-permute-start = (bf16[16,256]{1,0:T(8,128)(2,1)S(1)}, bf16[16,256]{1,0:T(8,128)(2,1)S(1)}, u32[]{:S(2)}, u32[]{:S(2)}) collective-permute-start(bf16[16,256]{1,0:T(8,128)(2,1)S(1)} %get-tuple-element.11), channel_id=1, source_target_pairs={{0,16},{16,32},{32,48},{48,64},{64,80},{80,96},{96,112},{112,128},... | collective-permute-start | bytes 24584 | tf_op jit(solution)/shard_map/ppermute | solution.py:360
